TPU v7x, 512 devices: a whole 4x8x8 slice. The times are simulated.
512 devices in a mesh: section: 32 (over z_lo, x, core), mp: 16 (over z_hi, y).
Axes of the slice: x: 4, y: 8, z: 8 (z_hi: 2, z_lo: 4; z = z_hi * 4 + z_lo), core: 2. Of those that a mesh axis runs over, the one named last changes fastest.
Arguments:
- queries: bfloat16 [32, 2, 64, 4096], P('section', None, None, 'mp'), may hold values from -48 to 48
- memory: bfloat16 [2, 128, 4096], P(None, None, 'section'), may hold values from -6 to 6
- key_weight: bfloat16 [32, 4096, 4096], P('section', None, 'mp'), may hold values from -0.09375 to 0.09375
- value_weight: bfloat16 [32, 4096, 4096], P('section', None, 'mp'), may hold values from -0.09375 to 0.09375
- context_grad: bfloat16 [32, 2, 64, 4096], P('section', None, None, 'mp'), may hold values from -6 to 6
Outputs:
- passed_context: bfloat16 [32, 2, 64, 4096], P('section', None, None, 'mp')
- passed_query_grad: bfloat16 [32, 2, 64, 4096], P('section', None, None, 'mp')
- memory_grad: float32 [2, 128, 4096], P(None, None, 'section')
All inputs are finite; a program needn't handle non-finite values.
Results may differ from a plain program's by a relative error of at most 0.012.
The roundings to bfloat16 on the way count: a program that leaves them out, or rounds other values in their place, can miss the bound.
Values may be sent and summed in bfloat16 or wider, within the bound.
No kernel may reach another device: no remote copies, remote signals or barrier semaphores. Data moves between devices by JAX's collectives and lax.ppermute only.
A program may use at most 64 MiB of HBM per device.

v0:
```python
import jax
import jax.numpy as jnp
from jax import lax
from jax.sharding import PartitionSpec as P

HEAD_DIM = 256


def from_behind(block, axis, distance):
    devices = range(lax.axis_size(axis))
    route = [(i - distance, i) for i in devices if i - distance in devices]
    return lax.ppermute(block, axis, route)


def attend_local(query_heads, key_heads, value_heads, grad_heads):
    scale = HEAD_DIM ** (-0.5)
    scores = (
        jnp.einsum("bqhd,bkhd->bhqk", query_heads, key_heads, preferred_element_type=jnp.float32)
        * scale
    )
    attention = jax.nn.softmax(scores, axis=-1)
    prob_low = attention.astype(jnp.bfloat16)
    context = jnp.einsum(
        "bhqk,bkhd->bqhd", prob_low, value_heads, preferred_element_type=jnp.float32
    ).astype(jnp.bfloat16)
    grad_probs = jnp.einsum(
        "bqhd,bkhd->bhqk", grad_heads, value_heads, preferred_element_type=jnp.float32
    )
    row_dot = jnp.sum(attention * grad_probs, axis=-1, keepdims=True)
    grad_scores = (attention * (grad_probs - row_dot) * scale).astype(jnp.bfloat16)
    query_grad = jnp.einsum(
        "bhqk,bkhd->bqhd", grad_scores, key_heads, preferred_element_type=jnp.float32
    ).astype(jnp.bfloat16)
    key_grad = jnp.einsum(
        "bhqk,bqhd->bkhd", grad_scores, query_heads, preferred_element_type=jnp.float32
    ).astype(jnp.bfloat16)
    value_grad = jnp.einsum(
        "bhqk,bqhd->bkhd", prob_low, grad_heads, preferred_element_type=jnp.float32
    ).astype(jnp.bfloat16)
    return (context, query_grad, key_grad, value_grad)


def per_device(queries, memory, key_weight, value_weight, context_grad):
    key_layer = key_weight[0]
    value_layer = value_weight[0]
    micro = memory.shape[0]
    mem_len = memory.shape[1]
    local_width = key_layer.shape[1]
    local_heads = local_width // HEAD_DIM
    width = key_layer.shape[0]
    portion = lax.all_gather(memory, "section", axis=2, tiled=True)
    key_sum = jnp.einsum("bmf,fh->bmh", portion, key_layer, preferred_element_type=jnp.float32)
    value_sum = jnp.einsum("bmf,fh->bmh", portion, value_layer, preferred_element_type=jnp.float32)
    key_rows = key_sum.astype(jnp.bfloat16)
    value_rows = value_sum.astype(jnp.bfloat16)
    dec_len = queries.shape[2]
    context, query_grad, key_grad, value_grad = attend_local(
        queries[0].reshape(micro, dec_len, local_heads, HEAD_DIM),
        key_rows.reshape(micro, mem_len, local_heads, HEAD_DIM),
        value_rows.reshape(micro, mem_len, local_heads, HEAD_DIM),
        context_grad[0].reshape(micro, dec_len, local_heads, HEAD_DIM),
    )
    passed_context = from_behind(context.reshape(1, micro, dec_len, local_width), "section", 1)
    passed_query_grad = from_behind(
        query_grad.reshape(1, micro, dec_len, local_width), "section", -1
    )
    contribution = jnp.dot(
        key_grad.reshape(micro * mem_len, local_width),
        key_layer.T,
        preferred_element_type=jnp.float32,
    )
    contribution = contribution + jnp.dot(
        value_grad.reshape(micro * mem_len, local_width),
        value_layer.T,
        preferred_element_type=jnp.float32,
    )
    contribution = contribution.reshape(micro, mem_len, width)
    head_total = lax.psum(contribution, "mp")
    memory_grad = lax.psum_scatter(head_total, "section", scatter_dimension=2, tiled=True)
    return (passed_context, passed_query_grad, memory_grad)


def solution(mesh):
    in_specs = (
        P("section", None, None, "mp"),
        P(None, None, "section"),
        P("section", None, "mp"),
        P("section", None, "mp"),
        P("section", None, None, "mp"),
    )
    out_specs = (
        P("section", None, None, "mp"),
        P("section", None, None, "mp"),
        P(None, None, "section"),
    )
    return jax.shard_map(
        per_device, mesh=mesh, in_specs=in_specs, out_specs=out_specs, check_vma=False
    )
```

profile of v0, /device:TPU:6, one launch (start us, length us, event | category | flops | bytes accessed | tf_op | source)
XLA Modules:
  0.0 445.5 jit_solution(17714392744709707946)
XLA Ops:
  7.2 0.0 copy-start
  7.2 0.0 all-gather.2.cloned.1.call-start
  7.2 0.7 all-gather.2.cloned.1.call-update
  7.9 0.0 copy-start.4
  7.9 0.0 reduce-scatter.2.cloned.1.call-start
  8.0 73.1 %all-gather.2.cloned.1.call-done = bf16[2,128,4096]{2,1,0:T(8,128)(2,1)} async-done(((bf16[2,128,128]{2,1,0:T(8,128)(2,1)}), bf16[2,128,4096]{2,1,0:T(8,128)(2,1)}) %all-gather.2.cloned.1.call-update) | async-done | bytes 2097168 | tf_op jit(solution)/shard_map/all_gather | solution.py:51
  81.0 0.0 copy-done
  81.0 0.0 copy-start.1
  81.0 0.0 copy-start.5
  81.0 2.4 fusion.12
  83.5 0.0 copy-done.4
  83.5 0.2 fusion.22
  83.7 0.4 fusion.40
  84.0 0.0 copy-done.1
  84.0 0.0 copy-done.5
  84.0 0.0 copy-start.3
  84.1 0.7 fusion.9
  84.8 0.1 copy-done.3
  84.9 0.2 convolution_bitcast_fusion
  85.0 0.4 convolution_convert_fusion
  85.4 0.4 convolution_convert_fusion.1
  85.9 0.0 copy-start.2
  85.9 0.7 fusion.4
  86.6 0.8 copy-done.2
  87.5 2.7 convolution_add_fusion
  90.2 0.0 reduce-scatter.2.cloned.1.call-update
  90.2 0.0 all-reduce.2.cloned.1.call-start
  90.3 0.3 fusion.16
  90.6 2.1 collective-permute-start
  92.7 133.5 %reduce-scatter.2.cloned.1.call-done = f32[2,128,128]{2,1,0:T(8,128)} async-done(((f32[2,128,4096]{2,1,0:T(8,128)}), f32[2,128,128]{2,1,0:T(8,128)}) %reduce-scatter.2.cloned.1.call-update) | async-done | bytes 131088 | tf_op jit(solution)/shard_map/reduce_scatter | solution.py:79
  226.2 0.0 all-reduce.2.cloned.1.call-update
  226.2 0.4 fusion.17
  226.6 2.8 collective-permute-start.1
  229.4 0.0 collective-permute-done
  229.4 1.9 collective-permute-done.1
  231.3 204.8 %all-reduce.2.cloned.1.call-done = f32[2,128,128]{2,1,0:T(8,128)} async-done(((f32[2,128,128]{2,1,0:T(8,128)}), f32[2,128,128]{2,1,0:T(8,128)}) %all-reduce.2.cloned.1.call-update) | async-done | bytes 131088 | tf_op jit(solution)/shard_map/psum | solution.py:78
  436.1 0.6 copy.11
  436.8 0.6 copy.12
  437.4 1.6 copy.13
Async XLA Ops:
  7.2 73.9 %copy-start = (bf16[1,4096,256]{2,1,0:T(8,128)(2,1)S(1)}, bf16[1,4096,256]{2,1,0:T(8,128)(2,1)}, u32[]{:S(2)}) copy-start(bf16[1,4096,256]{2,1,0:T(8,128)(2,1)} %param.7) | copy-start | bytes 6291460
  7.2 73.9 %all-gather.2.cloned.1.call-start = ((), (), s32[]{:S(2)}) async-start(), calls=%async_computation.1 | async-start | bytes 2162688 | tf_op jit(solution)/shard_map/all_gather | solution.py:51
  7.9 75.6 %copy-start.4 = (bf16[1,2,64,256]{3,2,1,0:T(8,128)(2,1)S(1)}, bf16[1,2,64,256]{3,2,1,0:T(8,128)(2,1)}, u32[]{:S(2)}) copy-start(bf16[1,2,64,256]{3,2,1,0:T(8,128)(2,1)} %param.5) | copy-start | bytes 196612
  7.9 218.3 %reduce-scatter.2.cloned.1.call-start = ((), (), s32[]{:S(2)}) async-start(), calls=%async_computation.2 | async-start | bytes 4325376 | tf_op jit(solution)/shard_map/reduce_scatter | solution.py:79
  81.0 3.0 copy-start.1
  81.0 3.0 copy-start.5
  84.0 0.8 copy-start.3
  85.9 1.6 copy-start.2
  90.2 345.9 %all-reduce.2.cloned.1.call-start = ((), (), s32[]{:S(2)}) async-start(), calls=%async_computation.3 | async-start | bytes 262144 | tf_op jit(solution)/shard_map/psum | solution.py:78
  90.6 138.9 %collective-permute-start = (bf16[1,2,64,256]{3,2,1,0:T(8,128)(2,1)S(1)}, bf16[1,2,64,256]{3,2,1,0:T(8,128)(2,1)S(1)}, u32[]{:S(2)}, u32[]{:S(2)}) collective-permute-start(bf16[1,2,64,256]{3,2,1,0:T(8,128)(2,1)S(1)} %fusion.16), channel_id=1, source_target_pairs={{0,16},{16,32},{32,48},{48,64},{64,80},{80,96},{96,112},{112,128},... | collective-permute-start | bytes 196616 | tf_op jit(solution)/shard_map/ppermute | solution.py:12
  226.6 4.7 %collective-permute-start.1 = (bf16[1,2,64,256]{3,2,1,0:T(8,128)(2,1)S(1)}, bf16[1,2,64,256]{3,2,1,0:T(8,128)(2,1)S(1)}, u32[]{:S(2)}, u32[]{:S(2)}) collective-permute-start(bf16[1,2,64,256]{3,2,1,0:T(8,128)(2,1)S(1)} %fusion.17), channel_id=1, source_target_pairs={{16,0},{32,16},{48,32},{64,48},{80,64},{96,80},{112,96},{128,112},... | collective-permute-start | bytes 196616 | tf_op jit(solution)/shard_map/ppermute | solution.py:12
Sparse Core Ops, SparseCore 0:
  10.1 70.9 all-gather.1
  90.3 135.8 reduce-scatter.1
  229.1 206.9 all-reduce.1
where the time goes:
time: 446 us; the launch traced here: 445 us
  waiting for transfers between devices  414 us (93%)
  between operations  13.9 us (3%)
  matrix products  8.41 us (2%)
  starting transfers between devices  5.09 us (1%)
    psum x1, waiting for transfers between devices, per_device(): head_total = lax.psum(contribution, 'mp')  205 us
    reduce_scatter x1, waiting for transfers between devices, per_device(): lax.psum_scatter(head_total, 'section', scatter_dimension=2, tiled=True)  133 us
    all_gather x1, waiting for transfers between devices, per_device(): portion = lax.all_gather(memory, 'section', axis=2, tiled=True)  73.1 us
  transfers between devices with their start and end apart: 5, of which 4 were waited for; matrix products, arithmetic and copies ran while one was open for 0% of the time, Pallas kernels for 0%

commit v1 on v0

v1 whole, which is shorter than its diff:
```python
import jax
import jax.numpy as jnp
from jax import lax
from jax.sharding import Mesh, PartitionSpec as P

HEAD_DIM = 256
AXES = ("z_lo", "x", "core", "z_hi", "y")
SIZES = (4, 4, 2, 2, 8)
CHIPS = 16
PART = 128


def index_of(z_lo, x, core, z_hi, y):
    return (((z_lo * 4 + x) * 2 + core) * 2 + z_hi) * 8 + y


def routes(step):
    pairs = []
    for chip in range(CHIPS):
        for core in range(2):
            to = step(chip, core)
            if to is None:
                continue
            for z_hi in range(2):
                for y in range(8):
                    pairs.append((
                        index_of(chip // 4, chip % 4, core, z_hi, y),
                        index_of(to[0] // 4, to[0] % 4, to[1], z_hi, y),
                    ))
    return pairs


def to_sibling(block):
    return lax.ppermute(block, AXES, routes(lambda chip, core: (chip, 1 - core)))


def to_next_chip(block):
    def step(chip, core):
        chip = chip + 1 if core == 1 else chip - 1
        return (chip, 1 - core) if 0 <= chip < CHIPS else None

    return lax.ppermute(block, AXES, routes(step))


def attend_local(query_heads, key_heads, value_heads, grad_heads):
    scale = HEAD_DIM ** (-0.5)
    scores = (
        jnp.einsum("bqd,bkd->bqk", query_heads, key_heads, preferred_element_type=jnp.float32)
        * scale
    )
    attention = jax.nn.softmax(scores, axis=-1)
    prob_low = attention.astype(jnp.bfloat16)
    context = jnp.einsum(
        "bqk,bkd->bqd", prob_low, value_heads, preferred_element_type=jnp.float32
    ).astype(jnp.bfloat16)
    grad_probs = jnp.einsum(
        "bqd,bkd->bqk", grad_heads, value_heads, preferred_element_type=jnp.float32
    )
    row_dot = jnp.sum(attention * grad_probs, axis=-1, keepdims=True)
    grad_scores = (attention * (grad_probs - row_dot) * scale).astype(jnp.bfloat16)
    query_grad = jnp.einsum(
        "bqk,bkd->bqd", grad_scores, key_heads, preferred_element_type=jnp.float32
    ).astype(jnp.bfloat16)
    key_grad = jnp.einsum(
        "bqk,bqd->bkd", grad_scores, query_heads, preferred_element_type=jnp.float32
    ).astype(jnp.bfloat16)
    value_grad = jnp.einsum(
        "bqk,bqd->bkd", prob_low, grad_heads, preferred_element_type=jnp.float32
    ).astype(jnp.bfloat16)
    return (context, query_grad, key_grad, value_grad)


def per_device(queries, memory, key_weight, value_weight, context_grad):
    core = lax.axis_index("core")
    key_layer = key_weight[0]
    value_layer = value_weight[0]
    own = memory.reshape(1, 256, PART)
    mine = lax.all_to_all(
        jnp.broadcast_to(own, (CHIPS, 256, PART)), ("z_lo", "x"), 0, 0, tiled=True
    )
    other = to_sibling(mine)
    first = jnp.where(core == 0, mine, other)
    second = jnp.where(core == 0, other, mine)
    portion = jnp.stack([first, second], axis=1)
    portion = portion.transpose(2, 0, 1, 3).reshape(256, 4096)
    key_rows = jnp.dot(portion, key_layer, preferred_element_type=jnp.float32)
    value_rows = jnp.dot(portion, value_layer, preferred_element_type=jnp.float32)
    key_rows = key_rows.astype(jnp.bfloat16).reshape(2, 128, 256)
    value_rows = value_rows.astype(jnp.bfloat16).reshape(2, 128, 256)
    context, query_grad, key_grad, value_grad = attend_local(
        queries[0], key_rows, value_rows, context_grad[0]
    )
    contribution = jnp.dot(
        key_grad.reshape(256, 256), key_layer.T, preferred_element_type=jnp.float32
    )
    contribution = contribution + jnp.dot(
        value_grad.reshape(256, 256), value_layer.T, preferred_element_type=jnp.float32
    )
    split = contribution.reshape(256, CHIPS, 2, PART)
    keep = lax.dynamic_index_in_dim(split, core, 2, keepdims=False).transpose(1, 0, 2)
    give = lax.dynamic_index_in_dim(split, 1 - core, 2, keepdims=False).transpose(1, 0, 2)
    inside = jnp.where(core == 0, context, query_grad).reshape(1, 256, PART)
    across = jnp.where(core == 0, query_grad, context)
    swapped = to_sibling(jnp.concatenate([give.astype(jnp.bfloat16), inside], axis=0))
    got_across = to_next_chip(across)
    got_inside = swapped[CHIPS].reshape(2, 64, 256)
    passed_context = jnp.where(core == 0, got_across, got_inside)
    passed_query_grad = jnp.where(core == 0, got_inside, got_across)
    chip_sum = (keep + swapped[:CHIPS].astype(jnp.float32)).astype(jnp.bfloat16)
    pieces = lax.all_to_all(
        chip_sum.reshape(CHIPS * 8, 32, PART), ("z_lo", "x", "y"), 0, 0, tiled=True
    )
    piece = jnp.sum(pieces.astype(jnp.float32), axis=0).astype(jnp.bfloat16)
    whole = lax.all_to_all(
        jnp.broadcast_to(piece[None], (16, 32, PART)), ("z_hi", "y"), 0, 0, tiled=True
    )
    halves = whole.reshape(2, 256, PART).astype(jnp.float32)
    memory_grad = (halves[0] + halves[1]).reshape(2, 128, PART)
    return (passed_context[None], passed_query_grad[None], memory_grad)


def solution(mesh):
    fine = Mesh(mesh.devices.reshape(SIZES), AXES)
    section = ("z_lo", "x", "core")
    mp = ("z_hi", "y")
    in_specs = (
        P(section, None, None, mp),
        P(None, None, section),
        P(section, None, mp),
        P(section, None, mp),
        P(section, None, None, mp),
    )
    out_specs = (
        P(section, None, None, mp),
        P(section, None, None, mp),
        P(None, None, section),
    )
    return jax.shard_map(
        per_device, mesh=fine, in_specs=in_specs, out_specs=out_specs, check_vma=False
    )
```

time: 446 us -> 142 us (0.32)
  waiting for transfers between devices: 414 us -> 41 us
  blocking collectives: 0 us -> 34.8 us
  starting transfers between devices: 5.09 us -> 28.8 us
  local copies, waits for them, and re-layouts: 3.81 us -> 20.4 us
  between operations: 13.9 us -> 0.85 us
  other arithmetic: 0.36 us -> 6.49 us
    psum x1 -> x0, waiting for transfers between devices: 205 us -> none  [per_device(): head_total = lax.psum(contribution, 'mp')]
    reduce_scatter x1 -> x0, waiting for transfers between devices: 133 us -> none  [per_device(): lax.psum_scatter(head_total, 'section', scatter_dimension=2, tiled=True)]
    all_gather x1 -> x0, waiting for transfers between devices: 73.1 us -> none  [per_device(): portion = lax.all_gather(memory, 'section', axis=2, tiled=True)]
    all_to_all x0 -> x2, waiting for transfers between devices: none -> 38.3 us  [the longest x1 27.3 us: per_device(): lax.all_to_all(chip_sum.reshape(CHIPS * 8, 32, PART), ('z_lo', 'x', 'y'),...]
    all_to_all x0 -> x1, blocking collectives: none -> 34.8 us  [per_device(): lax.all_to_all(jnp.broadcast_to(own, (CHIPS, 256, PART)), ('z_lo', 'x'),...]
    all_to_all x0 -> x2, starting transfers between devices: none -> 22.7 us  [the longest x1 13 us: per_device(): lax.all_to_all(chip_sum.reshape(CHIPS * 8, 32, PART), ('z_lo', 'x', 'y'),...]
    dynamic_slice x0 -> x2, local copies, waits for them, and re-layouts: none -> 8.68 us  [the longest x1 4.35 us: per_device(): lax.dynamic_index_in_dim(split, core, 2, keepdims=False).transpose(1, 0, 2)]
    reshape x0 -> x2, local copies, waits for them, and re-layouts: none -> 6.6 us  [the longest x1 6.58 us: per_device(): split = contribution.reshape(256, CHIPS, 2, PART)]
  transfers between devices with their start and end apart: 5 -> 5, of which waited for: 4 -> 3; matrix products, arithmetic and copies ran while one was open for 0% -> 5% of each run, Pallas kernels for 0% -> 0%
where the time goes in v1:
time: 142 us; the launch traced here: 139 us
  waiting for transfers between devices  41 us (29%)
  blocking collectives  34.8 us (25%)
  starting transfers between devices  28.8 us (20%)
  local copies, waits for them, and re-layouts  20.4 us (14%)
  matrix products  6.87 us (5%)
  other arithmetic  6.49 us (5%)
    all_to_all x1, blocking collectives, per_device(): lax.all_to_all(jnp.broadcast_to(own, (CHIPS, 256, PART)), ('z_lo', 'x'),...  34.8 us
    all_to_all x1, waiting for transfers between devices, per_device(): lax.all_to_all(chip_sum.reshape(CHIPS * 8, 32, PART), ('z_lo', 'x', 'y'),...  27.3 us
    all_to_all x1, starting transfers between devices, per_device(): lax.all_to_all(chip_sum.reshape(CHIPS * 8, 32, PART), ('z_lo', 'x', 'y'),...  13 us
    all_to_all x1, waiting for transfers between devices, per_device(): lax.all_to_all(jnp.broadcast_to(piece[None], (16, 32, PART)), ('z_hi', 'y...  10.9 us
    all_to_all x1, starting transfers between devices, per_device(): lax.all_to_all(jnp.broadcast_to(piece[None], (16, 32, PART)), ('z_hi', 'y...  9.67 us
    reshape x1, local copies, waits for them, and re-layouts, per_device(): split = contribution.reshape(256, CHIPS, 2, PART)  6.58 us
    dynamic_slice x1, local copies, waits for them, and re-layouts, per_device(): lax.dynamic_index_in_dim(split, core, 2, keepdims=False).transpose(1, 0, 2)  4.35 us
    dynamic_slice x1, local copies, waits for them, and re-layouts, per_device(): lax.dynamic_index_in_dim(split, 1 - core, 2, keepdims=False)  4.33 us
  transfers between devices with their start and end apart: 5, of which 3 were waited for; matrix products, arithmetic and copies ran while one was open for 5% of the time, Pallas kernels for 0%

profile of v1, /device:TPU:6, one launch (start us, length us, event | category | flops | bytes accessed | tf_op | source)
XLA Modules:
  0.0 139.2 jit_solution(11826010734267761978)
XLA Ops:
  0.6 0.0 copy-start
  0.6 1.1 copy.10
  1.7 0.1 broadcast_in_dim.11
  1.8 34.8 %all_to_all.15 = bf16[16,256,128]{1,2,0:T(8,128)(2,1)S(1)} all-to-all(bf16[16,256,128]{1,2,0:T(8,128)(2,1)S(1)} %broadcast_in_dim.11), channel_id=1, replica_groups=mesh['z_lo'=4,'x'=4,'core'=2,'z_hi'=2,'y'=8] {'z_lo','x'}, dimensions={0} | all-to-all | bytes 2097152 | tf_op jit(solution)/shard_map/all_to_all | solution.py:78
  36.6 1.9 %collective-permute-start = (bf16[16,256,128]{1,2,0:T(8,128)(2,1)S(1)}, bf16[16,256,128]{1,2,0:T(8,128)(2,1)}, u32[]{:S(2)}, u32[]{:S(2)}) collective-permute-start(bf16[16,256,128]{1,2,0:T(8,128)(2,1)S(1)} %all_to_all.15), channel_id=1, source_target_pairs={{0,16},{1,17},{2,18},{3,19},{4,20},{5,21},{6,22},{7,23},{8,24},{9,... | collective-permute-start | bytes 3145736 | tf_op jit(solution)/shard_map/ppermute | solution.py:34
  38.5 2.8 %collective-permute-done = bf16[16,256,128]{1,2,0:T(8,128)(2,1)} collective-permute-done((bf16[16,256,128]{1,2,0:T(8,128)(2,1)S(1)}, bf16[16,256,128]{1,2,0:T(8,128)(2,1)}, u32[]{:S(2)}, u32[]{:S(2)}) %collective-permute-start) | collective-permute-done | bytes 1048608 | tf_op jit(solution)/shard_map/ppermute | solution.py:34
  41.3 1.4 select_bitcast_fusion.1
  42.6 0.2 pad_maximum_fusion
  42.9 0.0 copy-done
  42.9 0.0 copy-start.1
  42.9 0.8 fusion.10
  43.7 0.8 copy-done.1
  44.5 0.0 copy-start.3
  44.5 0.0 copy-start.4
  44.5 0.8 fusion.13
  45.2 0.1 copy-done.3
  45.3 0.2 fusion.21
  45.5 0.4 fusion.40
  45.8 0.0 copy-done.4
  45.8 0.2 convolution_bitcast_fusion
  46.0 0.4 convolution_convert_fusion.3
  46.4 0.5 convolution_convert_fusion.1
  46.8 0.4 convolution_convert_fusion
  47.2 0.3 broadcast_select_fusion
  47.6 0.0 copy-start.2
  47.6 0.7 fusion.6
  48.3 0.8 copy-done.2
  49.1 2.8 %convolution_add_fusion = f32[256,4096]{1,0:T(8,128)} fusion(f32[256,4096]{1,0:T(8,128)S(1)} %fusion.6, bf16[256,256]{1,0:T(8,128)(2,1)S(1)} %bitcast.80, bf16[1,4096,256]{2,1,0:T(8,128)(2,1)S(1)} %copy-done.2), kind=kOutput, calls=%fused_computation.2 | convolution fusion | flops 537919488 | bytes 10616832 | tf_op jit(solution)/shard_map/dot_general | solution.py:96
  51.9 6.6 %reshape.52 = f32[256,16,2,128]{3,2,1,0:T(2,128)} reshape(f32[256,4096]{1,0:T(8,128)} %convolution_add_fusion) | data formatting | bytes 8388608 | tf_op jit(solution)/shard_map/reshape | solution.py:99
  58.5 4.3 %constant_dynamic-slice_fusion.1 = bf16[256,16,1,128]{3,2,1,0:T(2,128)(2,1)S(1)} fusion(f32[256,16,2,128]{3,2,1,0:T(2,128)} %reshape.52, s32[]{:T(128)S(6)} %select_n.44), kind=kLoop, calls=%fused_computation.51 | loop fusion | bytes 2097156 | tf_op jit(solution)/shard_map/jit(dynamic_index_in_dim)/dynamic_slice | solution.py:101
  62.8 0.7 copy.19
  63.5 0.1 pad_maximum_fusion.1
  63.6 2.0 %collective-permute-start.2 = (bf16[17,256,128]{2,1,0:T(8,128)(2,1)S(1)}, bf16[17,256,128]{2,1,0:T(8,128)(2,1)}, u32[]{:S(2)}, u32[]{:S(2)}) collective-permute-start(bf16[17,256,128]{2,1,0:T(8,128)(2,1)S(1)} %pad_maximum_fusion.1), channel_id=1, source_target_pairs={{0,16},{1,17},{2,18},{3,19},{4,20},{5,21},{6,22},{7,23},{8,24},{9,... | collective-permute-start | bytes 3342344 | tf_op jit(solution)/shard_map/ppermute | solution.py:34
  65.7 4.4 %constant_dynamic-slice_fusion = f32[256,16,1,128]{3,2,1,0:T(1,128)S(1)} fusion(f32[256,16,2,128]{3,2,1,0:T(2,128)} %reshape.52, s32[]{:T(128)S(6)} %select_n.48), kind=kLoop, calls=%fused_computation.50 | loop fusion | bytes 4194308 | tf_op jit(solution)/shard_map/jit(dynamic_index_in_dim)/dynamic_slice | solution.py:100
  70.0 0.0 collective-permute-done.2
  70.0 2.9 %fusion.2 = bf16[16,256,128]{2,1,0:T(8,128)(2,1)} fusion(f32[256,16,1,128]{3,2,1,0:T(1,128)S(1)} %constant_dynamic-slice_fusion, bf16[17,256,128]{2,1,0:T(8,128)(2,1)} %collective-permute-done.2), kind=kLoop, calls=%fused_computation.6 | loop fusion | flops 1572864 | bytes 4194304 | tf_op jit(solution)/shard_map/convert_element_type | solution.py:109
  72.9 13.0 %all-to-all-start.1 = ((bf16[128,32,128]{2,1,0:T(8,128)(2,1)}), bf16[128,32,128]{2,1,0:T(8,128)(2,1)S(1)}, u32[]{:S(2)}, u32[]{:S(2)}) async-start(bf16[128,32,128]{2,1,0:T(8,128)(2,1)} %bitcast.71), calls=%async_computation.1 | async-start | bytes 2097152 | tf_op jit(solution)/shard_map/all_to_all | solution.py:110
  86.0 2.1 %collective-permute-start.1 = (bf16[2,64,256]{2,1,0:T(8,128)(2,1)S(1)}, bf16[2,64,256]{2,1,0:T(8,128)(2,1)S(1)}, u32[]{:S(2)}, u32[]{:S(2)}) collective-permute-start(bf16[2,64,256]{2,1,0:T(8,128)(2,1)S(1)} %get-tuple-element.8), channel_id=1, source_target_pairs={{16,32},{17,33},{18,34},{19,35},{20,36},{21,37},{22,38},{23,39},{2... | collective-permute-start | bytes 196616 | tf_op jit(solution)/shard_map/ppermute | solution.py:42
  88.1 27.3 %all-to-all-done.1 = bf16[128,32,128]{2,1,0:T(8,128)(2,1)S(1)} async-done(((bf16[128,32,128]{2,1,0:T(8,128)(2,1)}), bf16[128,32,128]{2,1,0:T(8,128)(2,1)S(1)}, u32[]{:S(2)}, u32[]{:S(2)}) %all-to-all-start.1) | async-done | bytes 1048608 | tf_op jit(solution)/shard_map/all_to_all | solution.py:110
  115.4 0.2 reduce_sum.32
  115.6 0.7 broadcast_in_dim.26
  116.3 9.7 %all-to-all-start.2 = ((bf16[16,32,128]{2,1,0:T(8,128)(2,1)}), bf16[16,32,128]{2,1,0:T(8,128)(2,1)S(1)}, u32[]{:S(2)}, u32[]{:S(2)}) async-start(bf16[16,32,128]{2,1,0:T(8,128)(2,1)} %broadcast_in_dim.26), calls=%async_computation.2 | async-start | bytes 262144 | tf_op jit(solution)/shard_map/all_to_all | solution.py:114
  126.0 0.8 slice.18
  126.9 0.0 collective-permute-done.1
  126.9 0.7 select_bitcast_fusion.2
  127.5 10.9 %all-to-all-done.2 = bf16[16,32,128]{2,1,0:T(8,128)(2,1)S(1)} async-done(((bf16[16,32,128]{2,1,0:T(8,128)(2,1)}), bf16[16,32,128]{2,1,0:T(8,128)(2,1)S(1)}, u32[]{:S(2)}, u32[]{:S(2)}) %all-to-all-start.2) | async-done | bytes 131104 | tf_op jit(solution)/shard_map/all_to_all | solution.py:114
  138.5 0.7 slice_add_fusion
  (3 shorter events, 0.1 us)
Async XLA Ops:
  0.6 42.2 %copy-start = (bf16[1,4096,256]{2,1,0:T(8,128)(2,1)S(1)}, bf16[1,4096,256]{2,1,0:T(8,128)(2,1)}, u32[]{:S(2)}) copy-start(bf16[1,4096,256]{2,1,0:T(8,128)(2,1)} %param.7) | copy-start | bytes 6291460
  36.6 4.7 %collective-permute-start = (bf16[16,256,128]{1,2,0:T(8,128)(2,1)S(1)}, bf16[16,256,128]{1,2,0:T(8,128)(2,1)}, u32[]{:S(2)}, u32[]{:S(2)}) collective-permute-start(bf16[16,256,128]{1,2,0:T(8,128)(2,1)S(1)} %all_to_all.15), channel_id=1, source_target_pairs={{0,16},{1,17},{2,18},{3,19},{4,20},{5,21},{6,22},{7,23},{8,24},{9,... | collective-permute-start | bytes 3145736 | tf_op jit(solution)/shard_map/ppermute | solution.py:34
  42.9 1.6 %copy-start.1 = (bf16[1,4096,256]{2,1,0:T(8,128)(2,1)S(1)}, bf16[1,4096,256]{2,1,0:T(8,128)(2,1)}, u32[]{:S(2)}) copy-start(bf16[1,4096,256]{2,1,0:T(8,128)(2,1)} %param.8) | copy-start | bytes 6291460
  44.5 0.8 copy-start.3
  44.5 1.4 copy-start.4
  47.6 1.6 %copy-start.2 = (bf16[1,4096,256]{2,1,0:T(8,128)(2,1)S(1)}, bf16[1,4096,256]{2,1,0:T(8,128)(2,1)}, u32[]{:S(2)}) copy-start(bf16[1,4096,256]{2,1,0:T(8,128)(2,1)} %param.8) | copy-start | bytes 6291460
  63.6 6.4 %collective-permute-start.2 = (bf16[17,256,128]{2,1,0:T(8,128)(2,1)S(1)}, bf16[17,256,128]{2,1,0:T(8,128)(2,1)}, u32[]{:S(2)}, u32[]{:S(2)}) collective-permute-start(bf16[17,256,128]{2,1,0:T(8,128)(2,1)S(1)} %pad_maximum_fusion.1), channel_id=1, source_target_pairs={{0,16},{1,17},{2,18},{3,19},{4,20},{5,21},{6,22},{7,23},{8,24},{9,... | collective-permute-start | bytes 3342344 | tf_op jit(solution)/shard_map/ppermute | solution.py:34
  72.9 42.5 %all-to-all-start.1 = ((bf16[128,32,128]{2,1,0:T(8,128)(2,1)}), bf16[128,32,128]{2,1,0:T(8,128)(2,1)S(1)}, u32[]{:S(2)}, u32[]{:S(2)}) async-start(bf16[128,32,128]{2,1,0:T(8,128)(2,1)} %bitcast.71), calls=%async_computation.1 | async-start | bytes 2097152 | tf_op jit(solution)/shard_map/all_to_all | solution.py:110
  86.0 40.9 %collective-permute-start.1 = (bf16[2,64,256]{2,1,0:T(8,128)(2,1)S(1)}, bf16[2,64,256]{2,1,0:T(8,128)(2,1)S(1)}, u32[]{:S(2)}, u32[]{:S(2)}) collective-permute-start(bf16[2,64,256]{2,1,0:T(8,128)(2,1)S(1)} %get-tuple-element.8), channel_id=1, source_target_pairs={{16,32},{17,33},{18,34},{19,35},{20,36},{21,37},{22,38},{23,39},{2... | collective-permute-start | bytes 196616 | tf_op jit(solution)/shard_map/ppermute | solution.py:42
  116.3 22.2 %all-to-all-start.2 = ((bf16[16,32,128]{2,1,0:T(8,128)(2,1)}), bf16[16,32,128]{2,1,0:T(8,128)(2,1)S(1)}, u32[]{:S(2)}, u32[]{:S(2)}) async-start(bf16[16,32,128]{2,1,0:T(8,128)(2,1)} %broadcast_in_dim.26), calls=%async_computation.2 | async-start | bytes 262144 | tf_op jit(solution)/shard_map/all_to_all | solution.py:114

commit v2 on v1

v2 whole, which is shorter than its diff:
```python
import jax
import jax.numpy as jnp
from jax import lax
from jax.experimental import pallas as pl
from jax.experimental.pallas import tpu as pltpu
from jax.sharding import Mesh, PartitionSpec as P

HEAD_DIM = 256
AXES = ("z_lo", "x", "core", "z_hi", "y")
SIZES = (4, 4, 2, 2, 8)
CHIPS = 16
PART = 128


def index_of(z_lo, x, core, z_hi, y):
    return (((z_lo * 4 + x) * 2 + core) * 2 + z_hi) * 8 + y


def routes(step):
    pairs = []
    for chip in range(CHIPS):
        for core in range(2):
            to = step(chip, core)
            if to is None:
                continue
            for z_hi in range(2):
                for y in range(8):
                    pairs.append((
                        index_of(chip // 4, chip % 4, core, z_hi, y),
                        index_of(to[0] // 4, to[0] % 4, to[1], z_hi, y),
                    ))
    return pairs


def to_sibling(block):
    return lax.ppermute(block, AXES, routes(lambda chip, core: (chip, 1 - core)))


def to_next_chip(block):
    def step(chip, core):
        chip = chip + 1 if core == 1 else chip - 1
        return (chip, 1 - core) if 0 <= chip < CHIPS else None

    return lax.ppermute(block, AXES, routes(step))


def pair(ref, block, parity):
    low = ref[pl.ds(pl.multiple_of((4 * block + parity) * PART, PART), PART), :]
    high = ref[pl.ds(pl.multiple_of((4 * block + 2 + parity) * PART, PART), PART), :]
    return jnp.concatenate([low, high], axis=0)


def dot(a, b, contract):
    return lax.dot_general(a, b, (contract, ((), ())), preferred_element_type=jnp.float32)


def partial_rows(features, key_ref, value_ref, parity, key_sum, value_sum):
    for block in range(CHIPS // 2):
        tile = jnp.concatenate([features[2 * block], features[2 * block + 1]], axis=1)
        key_part = dot(tile, pair(key_ref, block, parity), ((1,), (0,)))
        value_part = dot(tile, pair(value_ref, block, parity), ((1,), (0,)))
        key_sum = key_part if key_sum is None else key_sum + key_part
        value_sum = value_part if value_sum is None else value_sum + value_part
    return key_sum, value_sum


def contribute(key_grad, value_grad, key_ref, value_ref, parity, block):
    part = dot(key_grad, pair(key_ref, block, parity), ((1,), (1,)))
    return part + dot(value_grad, pair(value_ref, block, parity), ((1,), (1,)))


def begin_kernel(core_ref, mine_ref, key_ref, value_ref, sum_ref):
    key_sum, value_sum = partial_rows(mine_ref, key_ref, value_ref, core_ref[0], None, None)
    sum_ref[0] = key_sum
    sum_ref[1] = value_sum


def attend_kernel(
    core_ref, other_ref, sum_ref, key_ref, value_ref, query_ref, grad_ref,
    give_ref, across_ref, grads_ref,
):
    core = core_ref[0]
    scale = HEAD_DIM ** (-0.5)
    key_sum, value_sum = partial_rows(
        other_ref, key_ref, value_ref, 1 - core, sum_ref[0], sum_ref[1]
    )
    key_rows = key_sum.astype(jnp.bfloat16)
    value_rows = value_sum.astype(jnp.bfloat16)
    contexts, query_grads = [], []
    for micro in range(2):
        keys = key_rows[micro * 128:(micro + 1) * 128]
        values = value_rows[micro * 128:(micro + 1) * 128]
        query = query_ref[micro]
        grad = grad_ref[micro]
        scores = dot(query, keys, ((1,), (1,))) * scale
        grad_probs = dot(grad, values, ((1,), (1,)))
        raised = jnp.exp(scores - jnp.max(scores, axis=-1, keepdims=True))
        attention = raised / jnp.sum(raised, axis=-1, keepdims=True)
        prob_low = attention.astype(jnp.bfloat16)
        row_dot = jnp.sum(attention * grad_probs, axis=-1, keepdims=True)
        grad_scores = (attention * (grad_probs - row_dot) * scale).astype(jnp.bfloat16)
        contexts.append(dot(prob_low, values, ((1,), (0,))).astype(jnp.bfloat16))
        query_grads.append(dot(grad_scores, keys, ((1,), (0,))).astype(jnp.bfloat16))
        rows = slice(micro * 128, (micro + 1) * 128)
        grads_ref[0, rows] = dot(grad_scores, query, ((0,), (0,))).astype(jnp.bfloat16)
        grads_ref[1, rows] = dot(prob_low, grad, ((0,), (0,))).astype(jnp.bfloat16)
    context = jnp.concatenate(contexts, axis=0)
    query_grad = jnp.concatenate(query_grads, axis=0)
    inside = jnp.where(core == 0, context, query_grad)
    across_ref[...] = jnp.where(core == 0, query_grad, context)
    give_ref[CHIPS, :128] = inside[:, :PART]
    give_ref[CHIPS, 128:] = inside[:, PART:]
    for block in range(CHIPS // 2):
        part = contribute(grads_ref[0], grads_ref[1], key_ref, value_ref, 1 - core, block)
        part = part.astype(jnp.bfloat16)
        give_ref[2 * block] = part[:, :PART]
        give_ref[2 * block + 1] = part[:, PART:]


def finish_kernel(core_ref, grads_ref, swapped_ref, key_ref, value_ref, total_ref):
    core = core_ref[0]
    for block in range(CHIPS // 2):
        part = contribute(grads_ref[0], grads_ref[1], key_ref, value_ref, core, block)
        low = part[:, :PART] + swapped_ref[2 * block].astype(jnp.float32)
        high = part[:, PART:] + swapped_ref[2 * block + 1].astype(jnp.float32)
        total_ref[2 * block] = low.astype(jnp.bfloat16)
        total_ref[2 * block + 1] = high.astype(jnp.bfloat16)


def call(kernel, outs, flops, *args):
    specs = [pl.BlockSpec(memory_space=pltpu.SMEM)]
    specs += [pl.BlockSpec(memory_space=pltpu.VMEM)] * (len(args) - 1)
    return pl.pallas_call(
        kernel,
        out_shape=outs,
        in_specs=specs,
        out_specs=[pl.BlockSpec(memory_space=pltpu.VMEM)] * len(outs),
        compiler_params=pltpu.CompilerParams(vmem_limit_bytes=32 * 2**20),
        cost_estimate=pl.CostEstimate(flops=flops, bytes_accessed=2**22, transcendentals=0),
    )(*args)


def per_device(queries, memory, key_weight, value_weight, context_grad):
    core = lax.axis_index("core")
    core_at = core.astype(jnp.int32).reshape(1)
    key_layer = key_weight[0]
    value_layer = value_weight[0]
    low, full = jnp.bfloat16, jnp.float32
    own = memory.reshape(1, 256, PART)
    mine = lax.all_to_all(
        jnp.broadcast_to(own, (CHIPS, 256, PART)), ("z_lo", "x"), 0, 0, tiled=True
    )
    other = to_sibling(mine)
    (sums,) = call(
        begin_kernel, [jax.ShapeDtypeStruct((2, 256, 256), full)], 2**29,
        core_at, mine, key_layer, value_layer,
    )
    give, across, grads = call(
        attend_kernel,
        [
            jax.ShapeDtypeStruct((CHIPS + 1, 256, PART), low),
            jax.ShapeDtypeStruct((128, 256), low),
            jax.ShapeDtypeStruct((2, 256, 256), low),
        ],
        2**30,
        core_at, other, sums, key_layer, value_layer, queries[0], context_grad[0],
    )
    swapped = to_sibling(give)
    got_across = to_next_chip(across)
    (chip_sum,) = call(
        finish_kernel, [jax.ShapeDtypeStruct((CHIPS, 256, PART), low)], 2**29,
        core_at, grads, swapped, key_layer, value_layer,
    )
    pieces = lax.all_to_all(
        chip_sum.reshape(CHIPS * 8, 32, PART), ("z_lo", "x", "y"), 0, 0, tiled=True
    )
    inside = swapped[CHIPS].reshape(2, 2, 64, PART)
    got_inside = jnp.concatenate([inside[0], inside[1]], axis=-1)
    got_across = got_across.reshape(2, 64, 256)
    passed_context = jnp.where(core == 0, got_across, got_inside)
    passed_query_grad = jnp.where(core == 0, got_inside, got_across)
    piece = jnp.sum(pieces.astype(full), axis=0).astype(low)
    whole = lax.all_to_all(
        jnp.broadcast_to(piece[None], (16, 32, PART)), ("z_hi", "y"), 0, 0, tiled=True
    )
    halves = whole.reshape(2, 256, PART).astype(full)
    memory_grad = (halves[0] + halves[1]).reshape(2, 128, PART)
    return (passed_context[None], passed_query_grad[None], memory_grad)


def solution(mesh):
    fine = Mesh(mesh.devices.reshape(SIZES), AXES)
    section = ("z_lo", "x", "core")
    mp = ("z_hi", "y")
    in_specs = (
        P(section, None, None, mp),
        P(None, None, section),
        P(section, None, mp),
        P(section, None, mp),
        P(section, None, None, mp),
    )
    out_specs = (
        P(section, None, None, mp),
        P(section, None, None, mp),
        P(None, None, section),
    )
    return jax.shard_map(
        per_device, mesh=fine, in_specs=in_specs, out_specs=out_specs, check_vma=False
    )
```

time: 142 us -> 120 us (0.85)
  local copies, waits for them, and re-layouts: 20.4 us -> 3.32 us
  matrix products: 6.87 us -> 0 us
  Pallas kernels: 0 us -> 5.98 us
  other arithmetic: 6.49 us -> 1.57 us
    dynamic_slice x2 -> x0, local copies, waits for them, and re-layouts: 8.68 us -> none  [the longest x1 4.35 us: per_device(): lax.dynamic_index_in_dim(split, core, 2, keepdims=False).transpose(1, 0, 2)]
    dot_general x10 -> x0, matrix products: 6.87 us -> none  [the longest x1 2.76 us: per_device(): jnp.dot(value_grad.reshape(256, 256), value_layer.T, preferred_element_ty...]
    reshape x2 -> x0, local copies, waits for them, and re-layouts: 6.6 us -> none  [the longest x1 6.58 us: per_device(): split = contribution.reshape(256, CHIPS, 2, PART)]
    pallas_call x0 -> x3, Pallas kernels: none -> 5.98 us  [call(): pl.pallas_call(kernel, out_shape=outs, in_specs=specs, out_specs=[pl.Bloc...]
    convert_element_type x2 -> x1, other arithmetic: 2.93 us -> 0.02 us  [per_device(): halves = whole.reshape(2, 256, PART).astype(full)]
    another operation x2 -> x0, other arithmetic: 1.56 us -> none  [per_device(): portion = jnp.stack([first, second], axis=1)]
  transfers between devices with their start and end apart: 5 -> 5, of which waited for: 3 -> 4; matrix products, arithmetic and copies ran while one was open for 5% -> 1% of each run, Pallas kernels for 0% -> 1%
where the time goes in v2:
time: 120 us; the launch traced here: 117 us
  waiting for transfers between devices  42.1 us (35%)
  blocking collectives  34.9 us (29%)
  starting transfers between devices  28.7 us (24%)
  Pallas kernels  5.98 us (5%)
  local copies, waits for them, and re-layouts  3.32 us (3%)
  other arithmetic  1.57 us (1%)
    all_to_all x1, blocking collectives, per_device(): lax.all_to_all(jnp.broadcast_to(own, (CHIPS, 256, PART)), ('z_lo', 'x'),...  34.9 us
    all_to_all x1, waiting for transfers between devices, per_device(): lax.all_to_all(chip_sum.reshape(CHIPS * 8, 32, PART), ('z_lo', 'x', 'y'),...  27.3 us
    all_to_all x1, starting transfers between devices, per_device(): lax.all_to_all(chip_sum.reshape(CHIPS * 8, 32, PART), ('z_lo', 'x', 'y'),...  13 us
    all_to_all x1, waiting for transfers between devices, per_device(): lax.all_to_all(jnp.broadcast_to(piece[None], (16, 32, PART)), ('z_hi', 'y...  11.8 us
    all_to_all x1, starting transfers between devices, per_device(): lax.all_to_all(jnp.broadcast_to(piece[None], (16, 32, PART)), ('z_hi', 'y...  9.66 us
    pallas_call x3, Pallas kernels, call(): pl.pallas_call(kernel, out_shape=outs, in_specs=specs, out_specs=[pl.Bloc...  5.98 us
    ppermute x2, starting transfers between devices, to_sibling(): lax.ppermute(block, AXES, routes(lambda chip, core: (chip, 1 - core)))  4.03 us
    ppermute x2, waiting for transfers between devices, to_sibling(): lax.ppermute(block, AXES, routes(lambda chip, core: (chip, 1 - core)))  2.95 us
  transfers between devices with their start and end apart: 5, of which 4 were waited for; matrix products, arithmetic and copies ran while one was open for 1% of the time, Pallas kernels for 1%

profile of v2, /device:TPU:6, one launch (start us, length us, event | category | flops | bytes accessed | tf_op | source)
XLA Modules:
  0.0 117.3 jit_solution(5433387530233292035)
XLA Ops:
  0.6 1.0 broadcast_in_dim.7
  1.7 0.0 copy-start
  1.7 34.9 %all_to_all.15.mine_ref = bf16[16,256,128]{2,1,0:T(8,128)(2,1)S(1)} all-to-all(bf16[16,256,128]{2,1,0:T(8,128)(2,1)S(1)} %broadcast_in_dim.7), channel_id=1, replica_groups=mesh['z_lo'=4,'x'=4,'core'=2,'z_hi'=2,'y'=8] {'z_lo','x'}, dimensions={0} | all-to-all | bytes 2097152 | tf_op jit(solution)/shard_map/all_to_all | solution.py:150
  36.6 1.9 %collective-permute-start = (bf16[16,256,128]{2,1,0:T(8,128)(2,1)S(1)}, bf16[16,256,128]{2,1,0:T(8,128)(2,1)}, u32[]{:S(2)}, u32[]{:S(2)}) collective-permute-start(bf16[16,256,128]{2,1,0:T(8,128)(2,1)S(1)} %all_to_all.15.mine_ref), channel_id=1, source_target_pairs={{0,16},{1,17},{2,18},{3,19},{4,20},{5,21},{6,22},{7,23},{8,24},{9,... | collective-permute-start | bytes 3145736 | tf_op jit(solution)/shard_map/ppermute | solution.py:36
  38.5 0.0 copy-done
  38.5 0.0 copy-start.1
  38.5 1.6 %copy-done.1 = bf16[1,4096,256]{2,1,0:T(8,128)(2,1)S(1)} copy-done((bf16[1,4096,256]{2,1,0:T(8,128)(2,1)S(1)}, bf16[1,4096,256]{2,1,0:T(8,128)(2,1)}, u32[]{:S(2)}) %copy-start.1) | copy-done | bytes 2097176
  40.1 0.0 copy-start.2
  40.1 0.0 copy-start.3
  40.1 0.7 shard_map.76.sum_ref
  40.8 0.4 collective-permute-done.other_ref
  41.3 0.0 copy-done.2
  41.3 0.0 copy-done.3
  41.3 3.5 %shard_map.77 = (bf16[17,256,128]{2,1,0:T(8,128)(2,1)S(1)}, bf16[128,256]{1,0:T(8,128)(2,1)S(1)}, bf16[2,256,256]{2,1,0:T(8,128)(2,1)S(1)}) custom-call(s32[1]{0:T(128)} %bitcast.core_ref, bf16[16,256,128]{2,1,0:T(8,128)(2,1)} %collective-permute-done.other_ref, f32[2,256,256]{2,1,0:T(8,128)S(1)} %shard_map.76.sum_ref, bf16[4096,256]{1,0:T(8,128)(2,1)S(1)} %bitcast.12, ...), custom_call_target="tpu_custom_call" | custom-call | flops 1073741824 | bytes 4194304 | tf_op jit(solution)/shard_map/pallas_call | solution.py:133
  44.8 2.1 %collective-permute-start.2 = (bf16[17,256,128]{2,1,0:T(8,128)(2,1)S(1)}, bf16[17,256,128]{2,1,0:T(8,128)(2,1)S(1)}, u32[]{:S(2)}, u32[]{:S(2)}) collective-permute-start(bf16[17,256,128]{2,1,0:T(8,128)(2,1)S(1)} %get-tuple-element.7), channel_id=1, source_target_pairs={{0,16},{1,17},{2,18},{3,19},{4,20},{5,21},{6,22},{7,23},{8,24},{9,... | collective-permute-start | bytes 3342344 | tf_op jit(solution)/shard_map/ppermute | solution.py:36
  46.9 2.5 %collective-permute-done.2.swapped_ref = bf16[17,256,128]{2,1,0:T(8,128)(2,1)S(1)} collective-permute-done((bf16[17,256,128]{2,1,0:T(8,128)(2,1)S(1)}, bf16[17,256,128]{2,1,0:T(8,128)(2,1)S(1)}, u32[]{:S(2)}, u32[]{:S(2)}) %collective-permute-start.2) | collective-permute-done | bytes 1114144 | tf_op jit(solution)/shard_map/ppermute | solution.py:36
  49.5 1.7 %shard_map.78 = bf16[16,256,128]{2,1,0:T(8,128)(2,1)} custom-call(s32[1]{0:T(128)} %bitcast.core_ref, bf16[2,256,256]{2,1,0:T(8,128)(2,1)S(1)} %get-tuple-element.8.grads_ref, bf16[17,256,128]{2,1,0:T(8,128)(2,1)S(1)} %collective-permute-done.2.swapped_ref, bf16[4096,256]{1,0:T(8,128)(2,1)S(1)} %bitcast.13, bf16[4096,256]{1,0:T(8,128)(2,1)S(1)} %bitcast.16), custom_call_target="tpu_custom_call" | custom-call | flops 536870912 | bytes 4194304 | tf_op jit(solution)/shard_map/pallas_call | solution.py:133
  51.2 13.0 %all-to-all-start.1 = ((bf16[128,32,128]{2,1,0:T(8,128)(2,1)}), bf16[128,32,128]{2,1,0:T(8,128)(2,1)S(1)}, u32[]{:S(2)}, u32[]{:S(2)}) async-start(bf16[128,32,128]{2,1,0:T(8,128)(2,1)} %bitcast.9), calls=%async_computation.1 | async-start | bytes 2097152 | tf_op jit(solution)/shard_map/all_to_all | solution.py:174
  64.2 2.0 %collective-permute-start.1 = (bf16[128,256]{1,0:T(8,128)(2,1)S(1)}, bf16[128,256]{1,0:T(8,128)(2,1)S(1)}, u32[]{:S(2)}, u32[]{:S(2)}) collective-permute-start(bf16[128,256]{1,0:T(8,128)(2,1)S(1)} %get-tuple-element.6), channel_id=1, source_target_pairs={{16,32},{17,33},{18,34},{19,35},{20,36},{21,37},{22,38},{23,39},{2... | collective-permute-start | bytes 196616 | tf_op jit(solution)/shard_map/ppermute | solution.py:44
  66.2 27.3 %all-to-all-done.1 = bf16[128,32,128]{2,1,0:T(8,128)(2,1)S(1)} async-done(((bf16[128,32,128]{2,1,0:T(8,128)(2,1)}), bf16[128,32,128]{2,1,0:T(8,128)(2,1)S(1)}, u32[]{:S(2)}, u32[]{:S(2)}) %all-to-all-start.1) | async-done | bytes 1048608 | tf_op jit(solution)/shard_map/all_to_all | solution.py:174
  93.5 0.2 reduce_sum.12
  93.7 0.7 broadcast_in_dim.8
  94.4 9.7 %all-to-all-start.2 = ((bf16[16,32,128]{2,1,0:T(8,128)(2,1)}), bf16[16,32,128]{2,1,0:T(8,128)(2,1)S(1)}, u32[]{:S(2)}, u32[]{:S(2)}) async-start(bf16[16,32,128]{2,1,0:T(8,128)(2,1)} %broadcast_in_dim.8), calls=%async_computation.2 | async-start | bytes 262144 | tf_op jit(solution)/shard_map/all_to_all | solution.py:183
  104.1 0.0 collective-permute-done.1
  104.1 0.7 broadcast_select_fusion
  104.8 11.8 %all-to-all-done.2 = bf16[16,32,128]{2,1,0:T(8,128)(2,1)S(1)} async-done(((bf16[16,32,128]{2,1,0:T(8,128)(2,1)}), bf16[16,32,128]{2,1,0:T(8,128)(2,1)S(1)}, u32[]{:S(2)}, u32[]{:S(2)}) %all-to-all-start.2) | async-done | bytes 131104 | tf_op jit(solution)/shard_map/all_to_all | solution.py:183
  116.6 0.7 slice_add_fusion
  (2 shorter events, 0.0 us)
Async XLA Ops:
  1.7 36.8 %copy-start = (bf16[1,4096,256]{2,1,0:T(8,128)(2,1)S(1)}, bf16[1,4096,256]{2,1,0:T(8,128)(2,1)}, u32[]{:S(2)}) copy-start(bf16[1,4096,256]{2,1,0:T(8,128)(2,1)} %param.7) | copy-start | bytes 6291460
  36.6 4.7 %collective-permute-start = (bf16[16,256,128]{2,1,0:T(8,128)(2,1)S(1)}, bf16[16,256,128]{2,1,0:T(8,128)(2,1)}, u32[]{:S(2)}, u32[]{:S(2)}) collective-permute-start(bf16[16,256,128]{2,1,0:T(8,128)(2,1)S(1)} %all_to_all.15.mine_ref), channel_id=1, source_target_pairs={{0,16},{1,17},{2,18},{3,19},{4,20},{5,21},{6,22},{7,23},{8,24},{9,... | collective-permute-start | bytes 3145736 | tf_op jit(solution)/shard_map/ppermute | solution.py:36
  38.5 1.6 %copy-start.1 = (bf16[1,4096,256]{2,1,0:T(8,128)(2,1)S(1)}, bf16[1,4096,256]{2,1,0:T(8,128)(2,1)}, u32[]{:S(2)}) copy-start(bf16[1,4096,256]{2,1,0:T(8,128)(2,1)} %param.8) | copy-start | bytes 6291460
  40.1 1.2 copy-start.2
  40.1 1.2 copy-start.3
  44.8 4.6 %collective-permute-start.2 = (bf16[17,256,128]{2,1,0:T(8,128)(2,1)S(1)}, bf16[17,256,128]{2,1,0:T(8,128)(2,1)S(1)}, u32[]{:S(2)}, u32[]{:S(2)}) collective-permute-start(bf16[17,256,128]{2,1,0:T(8,128)(2,1)S(1)} %get-tuple-element.7), channel_id=1, source_target_pairs={{0,16},{1,17},{2,18},{3,19},{4,20},{5,21},{6,22},{7,23},{8,24},{9,... | collective-permute-start | bytes 3342344 | tf_op jit(solution)/shard_map/ppermute | solution.py:36
  51.2 42.3 %all-to-all-start.1 = ((bf16[128,32,128]{2,1,0:T(8,128)(2,1)}), bf16[128,32,128]{2,1,0:T(8,128)(2,1)S(1)}, u32[]{:S(2)}, u32[]{:S(2)}) async-start(bf16[128,32,128]{2,1,0:T(8,128)(2,1)} %bitcast.9), calls=%async_computation.1 | async-start | bytes 2097152 | tf_op jit(solution)/shard_map/all_to_all | solution.py:174
  64.2 39.9 %collective-permute-start.1 = (bf16[128,256]{1,0:T(8,128)(2,1)S(1)}, bf16[128,256]{1,0:T(8,128)(2,1)S(1)}, u32[]{:S(2)}, u32[]{:S(2)}) collective-permute-start(bf16[128,256]{1,0:T(8,128)(2,1)S(1)} %get-tuple-element.6), channel_id=1, source_target_pairs={{16,32},{17,33},{18,34},{19,35},{20,36},{21,37},{22,38},{23,39},{2... | collective-permute-start | bytes 196616 | tf_op jit(solution)/shard_map/ppermute | solution.py:44
  94.4 22.2 %all-to-all-start.2 = ((bf16[16,32,128]{2,1,0:T(8,128)(2,1)}), bf16[16,32,128]{2,1,0:T(8,128)(2,1)S(1)}, u32[]{:S(2)}, u32[]{:S(2)}) async-start(bf16[16,32,128]{2,1,0:T(8,128)(2,1)} %broadcast_in_dim.8), calls=%async_computation.2 | async-start | bytes 262144 | tf_op jit(solution)/shard_map/all_to_all | solution.py:183

commit v3 on v2

--- a/solution.py
+++ b/solution.py
@@ -44,6 +44,10 @@
     return lax.ppermute(block, AXES, routes(step))
 
 
+def place(chip):
+    return chip % 4 * 4 + chip // 4
+
+
 def pair(ref, block, parity):
     low = ref[pl.ds(pl.multiple_of((4 * block + parity) * PART, PART), PART), :]
     high = ref[pl.ds(pl.multiple_of((4 * block + 2 + parity) * PART, PART), PART), :]
@@ -54,9 +58,15 @@
     return lax.dot_general(a, b, (contract, ((), ())), preferred_element_type=jnp.float32)
 
 
+def block_of(features, chip):
+    z_lo, x = chip // 4, chip % 4
+    return jnp.concatenate([features[x, z_lo], features[x, 4 + z_lo]], axis=0)
+
+
 def partial_rows(features, key_ref, value_ref, parity, key_sum, value_sum):
     for block in range(CHIPS // 2):
-        tile = jnp.concatenate([features[2 * block], features[2 * block + 1]], axis=1)
+        sides = [block_of(features, 2 * block), block_of(features, 2 * block + 1)]
+        tile = jnp.concatenate(sides, axis=1)
         key_part = dot(tile, pair(key_ref, block, parity), ((1,), (0,)))
         value_part = dot(tile, pair(value_ref, block, parity), ((1,), (0,)))
         key_sum = key_part if key_sum is None else key_sum + key_part
@@ -113,18 +123,22 @@
     for block in range(CHIPS // 2):
         part = contribute(grads_ref[0], grads_ref[1], key_ref, value_ref, 1 - core, block)
         part = part.astype(jnp.bfloat16)
-        give_ref[2 * block] = part[:, :PART]
-        give_ref[2 * block + 1] = part[:, PART:]
-
-
-def finish_kernel(core_ref, grads_ref, swapped_ref, key_ref, value_ref, total_ref):
-    core = core_ref[0]
+        give_ref[place(2 * block)] = part[:, :PART]
+        give_ref[place(2 * block + 1)] = part[:, PART:]
+
+
+def keep_kernel(core_ref, grads_ref, key_ref, value_ref, keep_ref):
     for block in range(CHIPS // 2):
-        part = contribute(grads_ref[0], grads_ref[1], key_ref, value_ref, core, block)
-        low = part[:, :PART] + swapped_ref[2 * block].astype(jnp.float32)
-        high = part[:, PART:] + swapped_ref[2 * block + 1].astype(jnp.float32)
-        total_ref[2 * block] = low.astype(jnp.bfloat16)
-        total_ref[2 * block + 1] = high.astype(jnp.bfloat16)
+        part = contribute(grads_ref[0], grads_ref[1], key_ref, value_ref, core_ref[0], block)
+        keep_ref[place(2 * block)] = part[:, :PART]
+        keep_ref[place(2 * block + 1)] = part[:, PART:]
+
+
+def add_kernel(core_ref, keep_ref, swapped_ref, total_ref):
+    for chip in range(CHIPS):
+        total_ref[chip] = (
+            keep_ref[chip] + swapped_ref[chip].astype(jnp.float32)
+        ).astype(jnp.bfloat16)
 
 
 def call(kernel, outs, flops, *args):
@@ -143,12 +157,14 @@
 def per_device(queries, memory, key_weight, value_weight, context_grad):
     core = lax.axis_index("core")
     core_at = core.astype(jnp.int32).reshape(1)
-    key_layer = key_weight[0]
-    value_layer = value_weight[0]
+    key_layer, value_layer = key_weight[0], value_weight[0]
     low, full = jnp.bfloat16, jnp.float32
-    own = memory.reshape(1, 256, PART)
+    half = lax.dynamic_slice_in_dim(memory, lax.axis_index("z_hi"), 1, 0)
+    column = lax.all_to_all(
+        jnp.broadcast_to(half, (8, 128, PART)), ("z_hi", "z_lo"), 0, 0, tiled=True
+    )
     mine = lax.all_to_all(
-        jnp.broadcast_to(own, (CHIPS, 256, PART)), ("z_lo", "x"), 0, 0, tiled=True
+        jnp.broadcast_to(column.reshape(1, 8, 128, PART), (4, 8, 128, PART)), "x", 0, 0, tiled=True
     )
     other = to_sibling(mine)
     (sums,) = call(
@@ -167,18 +183,25 @@
     )
     swapped = to_sibling(give)
     got_across = to_next_chip(across)
+    (keep,) = call(
+        keep_kernel, [jax.ShapeDtypeStruct((CHIPS, 256, PART), full)], 2**30,
+        core_at, grads, key_layer, value_layer,
+    )
     (chip_sum,) = call(
-        finish_kernel, [jax.ShapeDtypeStruct((CHIPS, 256, PART), low)], 2**29,
-        core_at, grads, swapped, key_layer, value_layer,
-    )
-    pieces = lax.all_to_all(
-        chip_sum.reshape(CHIPS * 8, 32, PART), ("z_lo", "x", "y"), 0, 0, tiled=True
-    )
+        add_kernel, [jax.ShapeDtypeStruct((CHIPS, 256, PART), low)], 2**20,
+        core_at, keep, swapped,
+    )
+    rows = lax.all_to_all(chip_sum.reshape(4, 4 * 256, PART), "x", 0, 0, tiled=True)
+    row_sum = jnp.sum(rows.astype(full), axis=0).astype(low)
+    pieces = lax.all_to_all(row_sum.reshape(32, 32, PART), ("z_lo", "y"), 0, 0, tiled=True)
     inside = swapped[CHIPS].reshape(2, 2, 64, PART)
     got_inside = jnp.concatenate([inside[0], inside[1]], axis=-1)
     got_across = got_across.reshape(2, 64, 256)
     passed_context = jnp.where(core == 0, got_across, got_inside)
     passed_query_grad = jnp.where(core == 0, got_inside, got_across)
+    pieces, passed_context, passed_query_grad = lax.optimization_barrier(
+        (pieces, passed_context, passed_query_grad)
+    )
     piece = jnp.sum(pieces.astype(full), axis=0).astype(low)
     whole = lax.all_to_all(
         jnp.broadcast_to(piece[None], (16, 32, PART)), ("z_hi", "y"), 0, 0, tiled=True

time: 120 us -> 113 us (0.942)
  blocking collectives: 34.9 us -> 74.5 us
  waiting for transfers between devices: 42.1 us -> 11.7 us
  starting transfers between devices: 28.7 us -> 13.9 us
    all_to_all x1 -> x4, blocking collectives: 34.9 us -> 74.5 us  [the longest x1 22.1 us: per_device(): lax.all_to_all(jnp.broadcast_to(half, (8, 128, PART)), ('z_hi', 'z_lo'),...]
    all_to_all x2 -> x1, waiting for transfers between devices: 39.1 us -> 5.83 us  [per_device(): lax.all_to_all(row_sum.reshape(32, 32, PART), ('z_lo', 'y'), 0, 0, tiled=...]
    all_to_all x2 -> x1, starting transfers between devices: 22.7 us -> 7.95 us  [per_device(): lax.all_to_all(row_sum.reshape(32, 32, PART), ('z_lo', 'y'), 0, 0, tiled=...]
    ppermute x1, waiting for transfers between devices: 0.01 us -> 3.64 us  [to_next_chip(): return lax.ppermute(block, AXES, routes(step))]
    unnamed x8 -> x10, local copies, waits for them, and re-layouts: 1.6 us -> 2.43 us
    pallas_call x3 -> x4, Pallas kernels: 5.98 us -> 5.2 us  [call(): pl.pallas_call(kernel, out_shape=outs, in_specs=specs, out_specs=[pl.Bloc...]
  transfers between devices with their start and end apart: 5 -> 4, of which waited for: 4 -> 4; matrix products, arithmetic and copies ran while one was open for 1% -> 1% of each run, Pallas kernels for 1% -> 1%
where the time goes in v3:
time: 113 us; the launch traced here: 111 us
  blocking collectives  74.5 us (66%)
  starting transfers between devices  13.9 us (12%)
  waiting for transfers between devices  11.7 us (10%)
  Pallas kernels  5.2 us (5%)
  local copies, waits for them, and re-layouts  2.72 us (2%)
  other arithmetic  2.32 us (2%)
    all_to_all x1, blocking collectives, per_device(): lax.all_to_all(jnp.broadcast_to(half, (8, 128, PART)), ('z_hi', 'z_lo'),...  22.1 us
    all_to_all x1, blocking collectives, per_device(): lax.all_to_all(jnp.broadcast_to(piece[None], (16, 32, PART)), ('z_hi', 'y...  18.4 us
    all_to_all x1, blocking collectives, per_device(): lax.all_to_all(chip_sum.reshape(4, 4 * 256, PART), 'x', 0, 0, tiled=True)  18.2 us
    all_to_all x1, blocking collectives, per_device(): lax.all_to_all(jnp.broadcast_to(column.reshape(1, 8, 128, PART), (4, 8, 1...  15.8 us
    all_to_all x1, starting transfers between devices, per_device(): lax.all_to_all(row_sum.reshape(32, 32, PART), ('z_lo', 'y'), 0, 0, tiled=...  7.95 us
    all_to_all x1, waiting for transfers between devices, per_device(): lax.all_to_all(row_sum.reshape(32, 32, PART), ('z_lo', 'y'), 0, 0, tiled=...  5.83 us
    pallas_call x4, Pallas kernels, call(): pl.pallas_call(kernel, out_shape=outs, in_specs=specs, out_specs=[pl.Bloc...  5.2 us
    ppermute x2, starting transfers between devices, to_sibling(): lax.ppermute(block, AXES, routes(lambda chip, core: (chip, 1 - core)))  4.03 us
  transfers between devices with their start and end apart: 4, of which 4 were waited for; matrix products, arithmetic and copies ran while one was open for 1% of the time, Pallas kernels for 1%

profile of v3, /device:TPU:6, one launch (start us, length us, event | category | flops | bytes accessed | tf_op | source)
XLA Modules:
  0.0 111.1 jit_solution(11022841967447601046)
XLA Ops:
  0.6 0.0 copy-start
  0.7 0.8 copy-done
  1.5 0.0 copy-start.1
  1.5 22.1 %all_to_all.25 = bf16[8,128,128]{2,1,0:T(8,128)(2,1)S(1)} all-to-all(bf16[8,128,128]{2,1,0:T(8,128)(2,1)S(1)} %broadcast_in_dim.25), channel_id=1, replica_groups=mesh['z_lo'=4,'x'=4,'core'=2,'z_hi'=2,'y'=8] {'z_hi','z_lo'}, dimensions={0} | all-to-all | bytes 524288 | tf_op jit(solution)/shard_map/all_to_all | solution.py:163
  23.6 0.2 broadcast_in_dim.26
  23.9 15.8 %all_to_all.26.mine_ref = bf16[4,8,128,128]{3,2,1,0:T(8,128)(2,1)S(1)} all-to-all(bf16[4,8,128,128]{3,2,1,0:T(8,128)(2,1)S(1)} %broadcast_in_dim.26), channel_id=1, replica_groups=mesh['z_lo'=4,'x'=4,'core'=2,'z_hi'=2,'y'=8] {'x'}, dimensions={0} | all-to-all | bytes 2097152 | tf_op jit(solution)/shard_map/all_to_all | solution.py:166
  39.7 1.9 %collective-permute-start = (bf16[4,8,128,128]{3,2,1,0:T(8,128)(2,1)S(1)}, bf16[4,8,128,128]{3,2,1,0:T(8,128)(2,1)}, u32[]{:S(2)}, u32[]{:S(2)}) collective-permute-start(bf16[4,8,128,128]{3,2,1,0:T(8,128)(2,1)S(1)} %all_to_all.26.mine_ref), channel_id=1, source_target_pairs={{0,16},{1,17},{2,18},{3,19},{4,20},{5,21},{6,22},{7,23},{8,24},{9,... | collective-permute-start | bytes 3145736 | tf_op jit(solution)/shard_map/ppermute | solution.py:36
  41.6 0.0 copy-done.1
  41.6 0.0 copy-start.2
  41.6 1.6 %copy-done.2 = bf16[1,4096,256]{2,1,0:T(8,128)(2,1)S(1)} copy-done((bf16[1,4096,256]{2,1,0:T(8,128)(2,1)S(1)}, bf16[1,4096,256]{2,1,0:T(8,128)(2,1)}, u32[]{:S(2)}) %copy-start.2) | copy-done | bytes 2097176
  43.2 0.0 copy-start.3
  43.2 0.0 copy-start.4
  43.2 0.7 shard_map.76.sum_ref
  43.9 0.4 collective-permute-done.other_ref
  44.4 0.0 copy-done.3
  44.4 0.0 copy-done.4
  44.4 3.5 %shard_map.77 = (bf16[17,256,128]{2,1,0:T(8,128)(2,1)S(1)}, bf16[128,256]{1,0:T(8,128)(2,1)S(1)}, bf16[2,256,256]{2,1,0:T(8,128)(2,1)S(1)}) custom-call(s32[1]{0:T(128)} %bitcast.core_ref, bf16[4,8,128,128]{3,2,1,0:T(8,128)(2,1)} %collective-permute-done.other_ref, f32[2,256,256]{2,1,0:T(8,128)S(1)} %shard_map.76.sum_ref, bf16[4096,256]{1,0:T(8,128)(2,1)S(1)} %bitcast.16, ...), custom_call_target="tpu_custom_call" | custom-call | flops 1073741824 | bytes 4194304 | tf_op jit(solution)/shard_map/pallas_call | solution.py:147
  47.9 2.1 %collective-permute-start.1 = (bf16[17,256,128]{2,1,0:T(8,128)(2,1)S(1)}, bf16[17,256,128]{2,1,0:T(8,128)(2,1)S(1)}, u32[]{:S(2)}, u32[]{:S(2)}) collective-permute-start(bf16[17,256,128]{2,1,0:T(8,128)(2,1)S(1)} %get-tuple-element.10), channel_id=1, source_target_pairs={{0,16},{1,17},{2,18},{3,19},{4,20},{5,21},{6,22},{7,23},{8,24},{9,... | collective-permute-start | bytes 3342344 | tf_op jit(solution)/shard_map/ppermute | solution.py:36
  50.0 0.8 shard_map.78.keep_ref
  50.8 1.8 %collective-permute-done.1.swapped_ref = bf16[17,256,128]{2,1,0:T(8,128)(2,1)S(1)} collective-permute-done((bf16[17,256,128]{2,1,0:T(8,128)(2,1)S(1)}, bf16[17,256,128]{2,1,0:T(8,128)(2,1)S(1)}, u32[]{:S(2)}, u32[]{:S(2)}) %collective-permute-start.1) | collective-permute-done | bytes 1114144 | tf_op jit(solution)/shard_map/ppermute | solution.py:36
  52.6 0.2 shard_map.79
  52.8 18.2 %all_to_all.27 = bf16[4,1024,128]{2,1,0:T(8,128)(2,1)S(1)} all-to-all(bf16[4,1024,128]{2,1,0:T(8,128)(2,1)S(1)} %bitcast.21), channel_id=1, replica_groups=mesh['z_lo'=4,'x'=4,'core'=2,'z_hi'=2,'y'=8] {'x'}, dimensions={0} | all-to-all | bytes 2097152 | tf_op jit(solution)/shard_map/all_to_all | solution.py:194
  71.0 0.9 reduce_sum.24
  71.8 8.0 %all-to-all-start.3 = ((bf16[32,32,128]{2,1,0:T(8,128)(2,1)}), bf16[32,32,128]{2,1,0:T(8,128)(2,1)S(1)}, u32[]{:S(2)}, u32[]{:S(2)}) async-start(bf16[32,32,128]{2,1,0:T(8,128)(2,1)} %bitcast.7), calls=%async_computation.3 | async-start | bytes 524288 | tf_op jit(solution)/shard_map/all_to_all | solution.py:196
  79.8 1.9 %collective-permute-start.2 = (bf16[128,256]{1,0:T(8,128)(2,1)S(1)}, bf16[128,256]{1,0:T(8,128)(2,1)S(1)}, u32[]{:S(2)}, u32[]{:S(2)}) collective-permute-start(bf16[128,256]{1,0:T(8,128)(2,1)S(1)} %get-tuple-element.11), channel_id=1, source_target_pairs={{16,32},{17,33},{18,34},{19,35},{20,36},{21,37},{22,38},{23,39},{2... | collective-permute-start | bytes 196616 | tf_op jit(solution)/shard_map/ppermute | solution.py:44
  81.8 3.6 %collective-permute-done.2 = bf16[128,256]{1,0:T(8,128)(2,1)S(1)} collective-permute-done((bf16[128,256]{1,0:T(8,128)(2,1)S(1)}, bf16[128,256]{1,0:T(8,128)(2,1)S(1)}, u32[]{:S(2)}, u32[]{:S(2)}) %collective-permute-start.2) | collective-permute-done | bytes 65568 | tf_op jit(solution)/shard_map/ppermute | solution.py:44
  85.4 0.7 broadcast_select_fusion
  86.1 5.8 %all-to-all-done.3 = bf16[32,32,128]{2,1,0:T(8,128)(2,1)S(1)} async-done(((bf16[32,32,128]{2,1,0:T(8,128)(2,1)}), bf16[32,32,128]{2,1,0:T(8,128)(2,1)S(1)}, u32[]{:S(2)}, u32[]{:S(2)}) %all-to-all-start.3) | async-done | bytes 262176 | tf_op jit(solution)/shard_map/all_to_all | solution.py:196
  91.9 0.1 reduce_sum.25
  92.0 18.4 %all_to_all.28 = bf16[16,32,128]{2,1,0:T(8,128)(2,1)S(1)} all-to-all(bf16[16,32,128]{2,1,0:T(8,128)(2,1)S(1)} %broadcast_in_dim.29), channel_id=1, replica_groups=mesh['z_lo'=4,'x'=4,'core'=2,'z_hi'=2,'y'=8] {'z_hi','y'}, dimensions={0} | all-to-all | bytes 262144 | tf_op jit(solution)/shard_map/all_to_all | solution.py:206
  110.4 0.7 slice_add_fusion
  (5 shorter events, 0.1 us)
Async XLA Ops:
  0.6 0.8 copy-start
  1.5 40.1 %copy-start.1 = (bf16[1,4096,256]{2,1,0:T(8,128)(2,1)S(1)}, bf16[1,4096,256]{2,1,0:T(8,128)(2,1)}, u32[]{:S(2)}) copy-start(bf16[1,4096,256]{2,1,0:T(8,128)(2,1)} %param.7) | copy-start | bytes 6291460
  39.7 4.7 %collective-permute-start = (bf16[4,8,128,128]{3,2,1,0:T(8,128)(2,1)S(1)}, bf16[4,8,128,128]{3,2,1,0:T(8,128)(2,1)}, u32[]{:S(2)}, u32[]{:S(2)}) collective-permute-start(bf16[4,8,128,128]{3,2,1,0:T(8,128)(2,1)S(1)} %all_to_all.26.mine_ref), channel_id=1, source_target_pairs={{0,16},{1,17},{2,18},{3,19},{4,20},{5,21},{6,22},{7,23},{8,24},{9,... | collective-permute-start | bytes 3145736 | tf_op jit(solution)/shard_map/ppermute | solution.py:36
  41.6 1.6 %copy-start.2 = (bf16[1,4096,256]{2,1,0:T(8,128)(2,1)S(1)}, bf16[1,4096,256]{2,1,0:T(8,128)(2,1)}, u32[]{:S(2)}) copy-start(bf16[1,4096,256]{2,1,0:T(8,128)(2,1)} %param.8) | copy-start | bytes 6291460
  43.2 1.2 %copy-start.3 = (bf16[1,2,64,256]{3,2,1,0:T(8,128)(2,1)S(1)}, bf16[1,2,64,256]{3,2,1,0:T(8,128)(2,1)}, u32[]{:S(2)}) copy-start(bf16[1,2,64,256]{3,2,1,0:T(8,128)(2,1)} %param.5) | copy-start | bytes 196612
  43.2 1.2 %copy-start.4 = (bf16[1,2,64,256]{3,2,1,0:T(8,128)(2,1)S(1)}, bf16[1,2,64,256]{3,2,1,0:T(8,128)(2,1)}, u32[]{:S(2)}) copy-start(bf16[1,2,64,256]{3,2,1,0:T(8,128)(2,1)} %param.9) | copy-start | bytes 196612
  47.9 4.6 %collective-permute-start.1 = (bf16[17,256,128]{2,1,0:T(8,128)(2,1)S(1)}, bf16[17,256,128]{2,1,0:T(8,128)(2,1)S(1)}, u32[]{:S(2)}, u32[]{:S(2)}) collective-permute-start(bf16[17,256,128]{2,1,0:T(8,128)(2,1)S(1)} %get-tuple-element.10), channel_id=1, source_target_pairs={{0,16},{1,17},{2,18},{3,19},{4,20},{5,21},{6,22},{7,23},{8,24},{9,... | collective-permute-start | bytes 3342344 | tf_op jit(solution)/shard_map/ppermute | solution.py:36
  71.8 20.1 %all-to-all-start.3 = ((bf16[32,32,128]{2,1,0:T(8,128)(2,1)}), bf16[32,32,128]{2,1,0:T(8,128)(2,1)S(1)}, u32[]{:S(2)}, u32[]{:S(2)}) async-start(bf16[32,32,128]{2,1,0:T(8,128)(2,1)} %bitcast.7), calls=%async_computation.3 | async-start | bytes 524288 | tf_op jit(solution)/shard_map/all_to_all | solution.py:196
  79.8 5.6 %collective-permute-start.2 = (bf16[128,256]{1,0:T(8,128)(2,1)S(1)}, bf16[128,256]{1,0:T(8,128)(2,1)S(1)}, u32[]{:S(2)}, u32[]{:S(2)}) collective-permute-start(bf16[128,256]{1,0:T(8,128)(2,1)S(1)} %get-tuple-element.11), channel_id=1, source_target_pairs={{16,32},{17,33},{18,34},{19,35},{20,36},{21,37},{22,38},{23,39},{2... | collective-permute-start | bytes 196616 | tf_op jit(solution)/shard_map/ppermute | solution.py:44

commit v4 on v3

--- a/solution.py
+++ b/solution.py
@@ -6,8 +6,8 @@
 from jax.sharding import Mesh, PartitionSpec as P
 
 HEAD_DIM = 256
-AXES = ("z_lo", "x", "core", "z_hi", "y")
-SIZES = (4, 4, 2, 2, 8)
+AXES = ("zq", "zb", "x", "core", "z_hi", "yq", "yb")
+SIZES = (2, 2, 4, 2, 2, 4, 2)
 CHIPS = 16
 PART = 128
 
@@ -44,10 +44,6 @@
     return lax.ppermute(block, AXES, routes(step))
 
 
-def place(chip):
-    return chip % 4 * 4 + chip // 4
-
-
 def pair(ref, block, parity):
     low = ref[pl.ds(pl.multiple_of((4 * block + parity) * PART, PART), PART), :]
     high = ref[pl.ds(pl.multiple_of((4 * block + 2 + parity) * PART, PART), PART), :]
@@ -60,7 +56,8 @@
 
 def block_of(features, chip):
     z_lo, x = chip // 4, chip % 4
-    return jnp.concatenate([features[x, z_lo], features[x, 4 + z_lo]], axis=0)
+    zb, zq = z_lo % 2, z_lo // 2
+    return jnp.concatenate([features[x, 0, zb, zq], features[x, 1, zb, zq]], axis=0)
 
 
 def partial_rows(features, key_ref, value_ref, parity, key_sum, value_sum):
@@ -123,22 +120,24 @@
     for block in range(CHIPS // 2):
         part = contribute(grads_ref[0], grads_ref[1], key_ref, value_ref, 1 - core, block)
         part = part.astype(jnp.bfloat16)
-        give_ref[place(2 * block)] = part[:, :PART]
-        give_ref[place(2 * block + 1)] = part[:, PART:]
+        give_ref[2 * block] = part[:, :PART]
+        give_ref[2 * block + 1] = part[:, PART:]
 
 
 def keep_kernel(core_ref, grads_ref, key_ref, value_ref, keep_ref):
     for block in range(CHIPS // 2):
         part = contribute(grads_ref[0], grads_ref[1], key_ref, value_ref, core_ref[0], block)
-        keep_ref[place(2 * block)] = part[:, :PART]
-        keep_ref[place(2 * block + 1)] = part[:, PART:]
+        keep_ref[2 * block] = part[:, :PART]
+        keep_ref[2 * block + 1] = part[:, PART:]
 
 
 def add_kernel(core_ref, keep_ref, swapped_ref, total_ref):
     for chip in range(CHIPS):
-        total_ref[chip] = (
-            keep_ref[chip] + swapped_ref[chip].astype(jnp.float32)
-        ).astype(jnp.bfloat16)
+        z_lo, x = chip // 4, chip % 4
+        total = keep_ref[chip] + swapped_ref[chip].astype(jnp.float32)
+        total = total.astype(jnp.bfloat16)
+        total_ref[x, 0, z_lo % 2, z_lo // 2] = total[:128]
+        total_ref[x, 1, z_lo % 2, z_lo // 2] = total[128:]
 
 
 def call(kernel, outs, flops, *args):
@@ -159,13 +158,12 @@
     core_at = core.astype(jnp.int32).reshape(1)
     key_layer, value_layer = key_weight[0], value_weight[0]
     low, full = jnp.bfloat16, jnp.float32
-    half = lax.dynamic_slice_in_dim(memory, lax.axis_index("z_hi"), 1, 0)
-    column = lax.all_to_all(
-        jnp.broadcast_to(half, (8, 128, PART)), ("z_hi", "z_lo"), 0, 0, tiled=True
-    )
+    half = lax.dynamic_slice_in_dim(memory, lax.axis_index("yb"), 1, 0)
+    column = lax.all_to_all(jnp.broadcast_to(half, (2, 128, PART)), "zq", 0, 0, tiled=True)
     mine = lax.all_to_all(
-        jnp.broadcast_to(column.reshape(1, 8, 128, PART), (4, 8, 128, PART)), "x", 0, 0, tiled=True
-    )
+        jnp.broadcast_to(column.reshape(1, 256, PART), (16, 256, PART)),
+        ("x", "yb", "zb"), 0, 0, tiled=True,
+    ).reshape(4, 2, 2, 2, 128, PART)
     other = to_sibling(mine)
     (sums,) = call(
         begin_kernel, [jax.ShapeDtypeStruct((2, 256, 256), full)], 2**29,
@@ -188,12 +186,17 @@
         core_at, grads, key_layer, value_layer,
     )
     (chip_sum,) = call(
-        add_kernel, [jax.ShapeDtypeStruct((CHIPS, 256, PART), low)], 2**20,
+        add_kernel, [jax.ShapeDtypeStruct((4, 2, 2, 2, 128, PART), low)], 2**20,
         core_at, keep, swapped,
     )
-    rows = lax.all_to_all(chip_sum.reshape(4, 4 * 256, PART), "x", 0, 0, tiled=True)
-    row_sum = jnp.sum(rows.astype(full), axis=0).astype(low)
-    pieces = lax.all_to_all(row_sum.reshape(32, 32, PART), ("z_lo", "y"), 0, 0, tiled=True)
+    pieces = lax.all_to_all(
+        chip_sum.reshape(16, 256, PART), ("x", "yb", "zb"), 0, 0, tiled=True
+    )
+    piece = jnp.sum(pieces.astype(full), axis=0).astype(low).reshape(1, 2, 128, PART)
+    pieces = lax.all_to_all(
+        jnp.broadcast_to(piece, (2, 2, 128, PART)).reshape(4, 128, PART),
+        ("z_hi", "zq"), 0, 0, tiled=True,
+    )
     inside = swapped[CHIPS].reshape(2, 2, 64, PART)
     got_inside = jnp.concatenate([inside[0], inside[1]], axis=-1)
     got_across = got_across.reshape(2, 64, 256)
@@ -204,17 +207,16 @@
     )
     piece = jnp.sum(pieces.astype(full), axis=0).astype(low)
     whole = lax.all_to_all(
-        jnp.broadcast_to(piece[None], (16, 32, PART)), ("z_hi", "y"), 0, 0, tiled=True
-    )
-    halves = whole.reshape(2, 256, PART).astype(full)
-    memory_grad = (halves[0] + halves[1]).reshape(2, 128, PART)
+        jnp.broadcast_to(piece[None], (8, 128, PART)), ("yq", "yb"), 0, 0, tiled=True
+    )
+    memory_grad = jnp.sum(whole.reshape(4, 2, 128, PART).astype(full), axis=0)
     return (passed_context[None], passed_query_grad[None], memory_grad)
 
 
 def solution(mesh):
     fine = Mesh(mesh.devices.reshape(SIZES), AXES)
-    section = ("z_lo", "x", "core")
-    mp = ("z_hi", "y")
+    section = ("zq", "zb", "x", "core")
+    mp = ("z_hi", "yq", "yb")
     in_specs = (
         P(section, None, None, mp),
         P(None, None, section),

time: 113 us -> 102 us (0.903)
  blocking collectives: 74.5 us -> 46.8 us
  waiting for transfers between devices: 11.7 us -> 22.5 us
  starting transfers between devices: 13.9 us -> 19.7 us
    all_to_all x4 -> x3, blocking collectives: 74.5 us -> 46.8 us  [the longest x1 20 us: per_device(): lax.all_to_all(jnp.broadcast_to(column.reshape(1, 256, PART), (16, 256, P...]
    all_to_all x1 -> x2, waiting for transfers between devices: 5.83 us -> 20.3 us  [the longest x1 12.2 us: per_device(): lax.all_to_all(chip_sum.reshape(16, 256, PART), ('x', 'yb', 'zb'), 0, 0,...]
    all_to_all x1 -> x2, starting transfers between devices: 7.95 us -> 13.4 us  [the longest x1 7.58 us: per_device(): lax.all_to_all(jnp.broadcast_to(piece, (2, 2, 128, PART)).reshape(4, 128,...]
    ppermute x1, waiting for transfers between devices: 3.64 us -> 0.01 us  [to_next_chip(): return lax.ppermute(block, AXES, routes(step))]
  transfers between devices with their start and end apart: 4 -> 5, of which waited for: 4 -> 4; matrix products, arithmetic and copies ran while one was open for 1% -> 1% of each run, Pallas kernels for 1% -> 1%
where the time goes in v4:
time: 102 us; the launch traced here: 101 us
  blocking collectives  46.8 us (46%)
  waiting for transfers between devices  22.5 us (22%)
  starting transfers between devices  19.7 us (19%)
  Pallas kernels  6.18 us (6%)
  local copies, waits for them, and re-layouts  3.34 us (3%)
  other arithmetic  1.53 us (2%)
    all_to_all x1, blocking collectives, per_device(): lax.all_to_all(jnp.broadcast_to(column.reshape(1, 256, PART), (16, 256, P...  20 us
    all_to_all x1, blocking collectives, per_device(): lax.all_to_all(jnp.broadcast_to(piece[None], (8, 128, PART)), ('yq', 'yb'...  16.5 us
    all_to_all x1, waiting for transfers between devices, per_device(): lax.all_to_all(chip_sum.reshape(16, 256, PART), ('x', 'yb', 'zb'), 0, 0,...  12.2 us
    all_to_all x1, blocking collectives, per_device(): lax.all_to_all(jnp.broadcast_to(half, (2, 128, PART)), 'zq', 0, 0, tiled=...  10.3 us
    all_to_all x1, waiting for transfers between devices, per_device(): lax.all_to_all(jnp.broadcast_to(piece, (2, 2, 128, PART)).reshape(4, 128,...  8.12 us
    all_to_all x1, starting transfers between devices, per_device(): lax.all_to_all(jnp.broadcast_to(piece, (2, 2, 128, PART)).reshape(4, 128,...  7.58 us
    pallas_call x4, Pallas kernels, call(): pl.pallas_call(kernel, out_shape=outs, in_specs=specs, out_specs=[pl.Bloc...  6.18 us
    all_to_all x1, starting transfers between devices, per_device(): lax.all_to_all(chip_sum.reshape(16, 256, PART), ('x', 'yb', 'zb'), 0, 0,...  5.8 us
  transfers between devices with their start and end apart: 5, of which 4 were waited for; matrix products, arithmetic and copies ran while one was open for 1% of the time, Pallas kernels for 1%

profile of v4, /device:TPU:6, one launch (start us, length us, event | category | flops | bytes accessed | tf_op | source)
XLA Modules:
  0.0 100.8 jit_solution(11392623040644354891)
XLA Ops:
  0.6 0.0 copy-start
  0.6 0.0 copy-start.1
  0.7 0.8 copy-done
  1.5 10.3 %all_to_all.25 = bf16[2,128,128]{2,1,0:T(8,128)(2,1)S(1)} all-to-all(bf16[2,128,128]{2,1,0:T(8,128)(2,1)S(1)} %broadcast_in_dim.34), channel_id=1, replica_groups=mesh['zq'=2,'zb'=2,'x'=4,'core'=2,'z_hi'=2,'yq'=4,'yb'=2] {'zq'}, dimensions={0} | all-to-all | bytes 131072 | tf_op jit(solution)/shard_map/all_to_all | solution.py:162
  11.8 0.2 broadcast_in_dim.36
  12.0 20.0 %all_to_all.26 = bf16[16,256,128]{2,1,0:T(8,128)(2,1)S(1)} all-to-all(bf16[16,256,128]{2,1,0:T(8,128)(2,1)S(1)} %broadcast_in_dim.36), channel_id=1, replica_groups=mesh['zq'=2,'zb'=2,'x'=4,'core'=2,'z_hi'=2,'yq'=4,'yb'=2] {'x','yb','zb'}, dimensions={0} | all-to-all | bytes 2097152 | tf_op jit(solution)/shard_map/all_to_all | solution.py:163
  32.0 1.9 %collective-permute-start = (bf16[4,2,2,2,128,128]{5,4,3,2,1,0:T(8,128)(2,1)S(1)}, bf16[4,2,2,2,128,128]{5,4,3,2,1,0:T(8,128)(2,1)}, u32[]{:S(2)}, u32[]{:S(2)}) collective-permute-start(bf16[4,2,2,2,128,128]{5,4,3,2,1,0:T(8,128)(2,1)S(1)} %bitcast.25), channel_id=1, source_target_pairs={{0,16},{1,17},{2,18},{3,19},{4,20},{5,21},{6,22},{7,23},{8,24},{9,... | collective-permute-start | bytes 3145736 | tf_op jit(solution)/shard_map/ppermute | solution.py:36
  33.9 0.0 copy-done.1
  33.9 0.0 copy-start.2
  33.9 1.6 %copy-done.2 = bf16[1,4096,256]{2,1,0:T(8,128)(2,1)S(1)} copy-done((bf16[1,4096,256]{2,1,0:T(8,128)(2,1)S(1)}, bf16[1,4096,256]{2,1,0:T(8,128)(2,1)}, u32[]{:S(2)}) %copy-start.2) | copy-done | bytes 2097176
  35.5 0.0 copy-start.3
  35.5 0.0 copy-start.4
  35.5 0.7 shard_map.76.sum_ref
  36.2 0.4 collective-permute-done.other_ref
  36.7 0.0 copy-done.3
  36.7 0.0 copy-done.4
  36.7 3.5 %shard_map.77 = (bf16[17,256,128]{2,1,0:T(8,128)(2,1)S(1)}, bf16[128,256]{1,0:T(8,128)(2,1)S(1)}, bf16[2,256,256]{2,1,0:T(8,128)(2,1)S(1)}) custom-call(s32[1]{0:T(128)} %bitcast.core_ref, bf16[4,2,2,2,128,128]{5,4,3,2,1,0:T(8,128)(2,1)} %collective-permute-done.other_ref, f32[2,256,256]{2,1,0:T(8,128)S(1)} %shard_map.76.sum_ref, ...), custom_call_target="tpu_custom_call" | custom-call | flops 1073741824 | bytes 4194304 | tf_op jit(solution)/shard_map/pallas_call | solution.py:146
  40.2 2.1 %collective-permute-start.1 = (bf16[17,256,128]{2,1,0:T(8,128)(2,1)S(1)}, bf16[17,256,128]{2,1,0:T(8,128)(2,1)S(1)}, u32[]{:S(2)}, u32[]{:S(2)}) collective-permute-start(bf16[17,256,128]{2,1,0:T(8,128)(2,1)S(1)} %get-tuple-element.10), channel_id=1, source_target_pairs={{0,16},{1,17},{2,18},{3,19},{4,20},{5,21},{6,22},{7,23},{8,24},{9,... | collective-permute-start | bytes 3342344 | tf_op jit(solution)/shard_map/ppermute | solution.py:36
  42.3 0.8 shard_map.78.keep_ref
  43.1 1.8 %collective-permute-done.1.swapped_ref = bf16[17,256,128]{2,1,0:T(8,128)(2,1)S(1)} collective-permute-done((bf16[17,256,128]{2,1,0:T(8,128)(2,1)S(1)}, bf16[17,256,128]{2,1,0:T(8,128)(2,1)S(1)}, u32[]{:S(2)}, u32[]{:S(2)}) %collective-permute-start.1) | collective-permute-done | bytes 1114144 | tf_op jit(solution)/shard_map/ppermute | solution.py:36
  44.9 1.2 %shard_map.79 = bf16[4,2,2,2,128,128]{5,4,3,2,1,0:T(8,128)(2,1)} custom-call(s32[1]{0:T(128)} %bitcast.core_ref, f32[16,256,128]{2,1,0:T(8,128)S(1)} %shard_map.78.keep_ref, bf16[17,256,128]{2,1,0:T(8,128)(2,1)S(1)} %collective-permute-done.1.swapped_ref), custom_call_target="tpu_custom_call" | custom-call | flops 1048576 | bytes 4194304 | tf_op jit(solution)/shard_map/pallas_call | solution.py:146
  46.1 5.8 %all-to-all-start.2 = ((bf16[16,256,128]{2,1,0:T(8,128)(2,1)}), bf16[16,256,128]{2,1,0:T(8,128)(2,1)S(1)}, u32[]{:S(2)}, u32[]{:S(2)}) async-start(bf16[16,256,128]{2,1,0:T(8,128)(2,1)} %bitcast.8), calls=%async_computation.2 | async-start | bytes 2097152 | tf_op jit(solution)/shard_map/all_to_all | solution.py:192
  51.9 2.3 %collective-permute-start.2 = (bf16[128,256]{1,0:T(8,128)(2,1)S(1)}, bf16[128,256]{1,0:T(8,128)(2,1)S(1)}, u32[]{:S(2)}, u32[]{:S(2)}) collective-permute-start(bf16[128,256]{1,0:T(8,128)(2,1)S(1)} %get-tuple-element.11), channel_id=1, source_target_pairs={{16,32},{17,33},{18,34},{19,35},{20,36},{21,37},{22,38},{23,39},{2... | collective-permute-start | bytes 196616 | tf_op jit(solution)/shard_map/ppermute | solution.py:44
  54.1 12.2 %all-to-all-done.2 = bf16[16,256,128]{2,1,0:T(8,128)(2,1)S(1)} async-done(((bf16[16,256,128]{2,1,0:T(8,128)(2,1)}), bf16[16,256,128]{2,1,0:T(8,128)(2,1)S(1)}, u32[]{:S(2)}, u32[]{:S(2)}) %all-to-all-start.2) | async-done | bytes 1048608 | tf_op jit(solution)/shard_map/all_to_all | solution.py:192
  66.4 0.1 reduce_sum.33
  66.5 0.7 broadcast_in_dim.38
  67.2 7.6 %all-to-all-start.3 = ((bf16[4,128,128]{2,1,0:T(8,128)(2,1)}), bf16[4,128,128]{2,1,0:T(8,128)(2,1)S(1)}, u32[]{:S(2)}, u32[]{:S(2)}) async-start(bf16[4,128,128]{2,1,0:T(8,128)(2,1)} %bitcast.10), calls=%async_computation.3 | async-start | bytes 262144 | tf_op jit(solution)/shard_map/all_to_all | solution.py:196
  74.8 0.0 collective-permute-done.2
  74.8 0.7 broadcast_select_fusion
  75.4 8.1 %all-to-all-done.3 = bf16[4,128,128]{2,1,0:T(8,128)(2,1)S(1)} async-done(((bf16[4,128,128]{2,1,0:T(8,128)(2,1)}), bf16[4,128,128]{2,1,0:T(8,128)(2,1)S(1)}, u32[]{:S(2)}, u32[]{:S(2)}) %all-to-all-start.3) | async-done | bytes 131104 | tf_op jit(solution)/shard_map/all_to_all | solution.py:196
  83.6 16.5 %all_to_all.27 = bf16[8,128,128]{2,1,0:T(8,128)(2,1)S(1)} all-to-all(bf16[8,128,128]{2,1,0:T(8,128)(2,1)S(1)} %broadcast_in_dim.41), channel_id=1, replica_groups=mesh['zq'=2,'zb'=2,'x'=4,'core'=2,'z_hi'=2,'yq'=4,'yb'=2] {'yq','yb'}, dimensions={0} | all-to-all | bytes 524288 | tf_op jit(solution)/shard_map/all_to_all | solution.py:209
  100.1 0.7 convert_reduce_fusion
  (5 shorter events, 0.1 us)
Async XLA Ops:
  0.6 0.8 copy-start
  0.6 33.3 %copy-start.1 = (bf16[1,4096,256]{2,1,0:T(8,128)(2,1)S(1)}, bf16[1,4096,256]{2,1,0:T(8,128)(2,1)}, u32[]{:S(2)}) copy-start(bf16[1,4096,256]{2,1,0:T(8,128)(2,1)} %param.7) | copy-start | bytes 6291460
  32.0 4.7 %collective-permute-start = (bf16[4,2,2,2,128,128]{5,4,3,2,1,0:T(8,128)(2,1)S(1)}, bf16[4,2,2,2,128,128]{5,4,3,2,1,0:T(8,128)(2,1)}, u32[]{:S(2)}, u32[]{:S(2)}) collective-permute-start(bf16[4,2,2,2,128,128]{5,4,3,2,1,0:T(8,128)(2,1)S(1)} %bitcast.25), channel_id=1, source_target_pairs={{0,16},{1,17},{2,18},{3,19},{4,20},{5,21},{6,22},{7,23},{8,24},{9,... | collective-permute-start | bytes 3145736 | tf_op jit(solution)/shard_map/ppermute | solution.py:36
  33.9 1.6 %copy-start.2 = (bf16[1,4096,256]{2,1,0:T(8,128)(2,1)S(1)}, bf16[1,4096,256]{2,1,0:T(8,128)(2,1)}, u32[]{:S(2)}) copy-start(bf16[1,4096,256]{2,1,0:T(8,128)(2,1)} %param.8) | copy-start | bytes 6291460
  35.5 1.2 %copy-start.3 = (bf16[1,2,64,256]{3,2,1,0:T(8,128)(2,1)S(1)}, bf16[1,2,64,256]{3,2,1,0:T(8,128)(2,1)}, u32[]{:S(2)}) copy-start(bf16[1,2,64,256]{3,2,1,0:T(8,128)(2,1)} %param.5) | copy-start | bytes 196612
  35.5 1.2 %copy-start.4 = (bf16[1,2,64,256]{3,2,1,0:T(8,128)(2,1)S(1)}, bf16[1,2,64,256]{3,2,1,0:T(8,128)(2,1)}, u32[]{:S(2)}) copy-start(bf16[1,2,64,256]{3,2,1,0:T(8,128)(2,1)} %param.9) | copy-start | bytes 196612
  40.2 4.6 %collective-permute-start.1 = (bf16[17,256,128]{2,1,0:T(8,128)(2,1)S(1)}, bf16[17,256,128]{2,1,0:T(8,128)(2,1)S(1)}, u32[]{:S(2)}, u32[]{:S(2)}) collective-permute-start(bf16[17,256,128]{2,1,0:T(8,128)(2,1)S(1)} %get-tuple-element.10), channel_id=1, source_target_pairs={{0,16},{1,17},{2,18},{3,19},{4,20},{5,21},{6,22},{7,23},{8,24},{9,... | collective-permute-start | bytes 3342344 | tf_op jit(solution)/shard_map/ppermute | solution.py:36
  46.1 20.3 %all-to-all-start.2 = ((bf16[16,256,128]{2,1,0:T(8,128)(2,1)}), bf16[16,256,128]{2,1,0:T(8,128)(2,1)S(1)}, u32[]{:S(2)}, u32[]{:S(2)}) async-start(bf16[16,256,128]{2,1,0:T(8,128)(2,1)} %bitcast.8), calls=%async_computation.2 | async-start | bytes 2097152 | tf_op jit(solution)/shard_map/all_to_all | solution.py:192
  51.9 22.9 %collective-permute-start.2 = (bf16[128,256]{1,0:T(8,128)(2,1)S(1)}, bf16[128,256]{1,0:T(8,128)(2,1)S(1)}, u32[]{:S(2)}, u32[]{:S(2)}) collective-permute-start(bf16[128,256]{1,0:T(8,128)(2,1)S(1)} %get-tuple-element.11), channel_id=1, source_target_pairs={{16,32},{17,33},{18,34},{19,35},{20,36},{21,37},{22,38},{23,39},{2... | collective-permute-start | bytes 196616 | tf_op jit(solution)/shard_map/ppermute | solution.py:44
  67.2 16.4 %all-to-all-start.3 = ((bf16[4,128,128]{2,1,0:T(8,128)(2,1)}), bf16[4,128,128]{2,1,0:T(8,128)(2,1)S(1)}, u32[]{:S(2)}, u32[]{:S(2)}) async-start(bf16[4,128,128]{2,1,0:T(8,128)(2,1)} %bitcast.10), calls=%async_computation.3 | async-start | bytes 262144 | tf_op jit(solution)/shard_map/all_to_all | solution.py:196

commit v5 on v4

--- a/solution.py
+++ b/solution.py
@@ -202,9 +202,6 @@
     got_across = got_across.reshape(2, 64, 256)
     passed_context = jnp.where(core == 0, got_across, got_inside)
     passed_query_grad = jnp.where(core == 0, got_inside, got_across)
-    pieces, passed_context, passed_query_grad = lax.optimization_barrier(
-        (pieces, passed_context, passed_query_grad)
-    )
     piece = jnp.sum(pieces.astype(full), axis=0).astype(low)
     whole = lax.all_to_all(
         jnp.broadcast_to(piece[None], (8, 128, PART)), ("yq", "yb"), 0, 0, tiled=True

time: 102 us -> 99.9 us (0.979)
  blocking collectives: 46.8 us -> 65.8 us
  waiting for transfers between devices: 22.5 us -> 10.1 us
  starting transfers between devices: 19.7 us -> 12.1 us
    all_to_all x1 -> x2, blocking collectives: 16.5 us -> 35.5 us  [the longest x1 19.3 us: per_device(): lax.all_to_all(chip_sum.reshape(16, 256, PART), ('x', 'yb', 'zb'), 0, 0,...]
    all_to_all x2 -> x1, waiting for transfers between devices: 20.3 us -> 4.23 us  [per_device(): lax.all_to_all(jnp.broadcast_to(piece[None], (8, 128, PART)), ('yq', 'yb'...]
    all_to_all x2 -> x1, starting transfers between devices: 13.4 us -> 6.2 us  [per_device(): lax.all_to_all(jnp.broadcast_to(piece[None], (8, 128, PART)), ('yq', 'yb'...]
    ppermute x1, waiting for transfers between devices: 0.01 us -> 3.64 us  [to_next_chip(): return lax.ppermute(block, AXES, routes(step))]
  transfers between devices with their start and end apart: 5 -> 4, of which waited for: 4 -> 4; matrix products, arithmetic and copies ran while one was open for 1% -> 1% of each run, Pallas kernels for 1% -> 1%
where the time goes in v5:
time: 99.9 us; the launch traced here: 98.9 us
  blocking collectives  65.8 us (66%)
  starting transfers between devices  12.1 us (12%)
  waiting for transfers between devices  10.1 us (10%)
  Pallas kernels  5.2 us (5%)
  local copies, waits for them, and re-layouts  3.38 us (3%)
  other arithmetic  1.53 us (2%)
    all_to_all x1, blocking collectives, per_device(): lax.all_to_all(jnp.broadcast_to(column.reshape(1, 256, PART), (16, 256, P...  20 us
    all_to_all x1, blocking collectives, per_device(): lax.all_to_all(chip_sum.reshape(16, 256, PART), ('x', 'yb', 'zb'), 0, 0,...  19.3 us
    all_to_all x1, blocking collectives, per_device(): lax.all_to_all(jnp.broadcast_to(piece, (2, 2, 128, PART)).reshape(4, 128,...  16.2 us
    all_to_all x1, blocking collectives, per_device(): lax.all_to_all(jnp.broadcast_to(half, (2, 128, PART)), 'zq', 0, 0, tiled=...  10.3 us
    all_to_all x1, starting transfers between devices, per_device(): lax.all_to_all(jnp.broadcast_to(piece[None], (8, 128, PART)), ('yq', 'yb'...  6.2 us
    pallas_call x4, Pallas kernels, call(): pl.pallas_call(kernel, out_shape=outs, in_specs=specs, out_specs=[pl.Bloc...  5.2 us
    all_to_all x1, waiting for transfers between devices, per_device(): lax.all_to_all(jnp.broadcast_to(piece[None], (8, 128, PART)), ('yq', 'yb'...  4.23 us
    ppermute x2, starting transfers between devices, to_sibling(): lax.ppermute(block, AXES, routes(lambda chip, core: (chip, 1 - core)))  4.03 us
  transfers between devices with their start and end apart: 4, of which 4 were waited for; matrix products, arithmetic and copies ran while one was open for 1% of the time, Pallas kernels for 1%

profile of v5, /device:TPU:6, one launch (start us, length us, event | category | flops | bytes accessed | tf_op | source)
XLA Modules:
  0.0 98.9 jit_solution(18070807896230030523)
XLA Ops:
  0.6 0.0 copy-start
  0.6 0.0 copy-start.1
  0.7 0.8 copy-done
  1.5 10.3 %all_to_all.25 = bf16[2,128,128]{2,1,0:T(8,128)(2,1)S(1)} all-to-all(bf16[2,128,128]{2,1,0:T(8,128)(2,1)S(1)} %broadcast_in_dim.30), channel_id=1, replica_groups=mesh['zq'=2,'zb'=2,'x'=4,'core'=2,'z_hi'=2,'yq'=4,'yb'=2] {'zq'}, dimensions={0} | all-to-all | bytes 131072 | tf_op jit(solution)/shard_map/all_to_all | solution.py:162
  11.8 0.2 broadcast_in_dim.32
  12.0 20.0 %all_to_all.26 = bf16[16,256,128]{2,1,0:T(8,128)(2,1)S(1)} all-to-all(bf16[16,256,128]{2,1,0:T(8,128)(2,1)S(1)} %broadcast_in_dim.32), channel_id=1, replica_groups=mesh['zq'=2,'zb'=2,'x'=4,'core'=2,'z_hi'=2,'yq'=4,'yb'=2] {'x','yb','zb'}, dimensions={0} | all-to-all | bytes 2097152 | tf_op jit(solution)/shard_map/all_to_all | solution.py:163
  32.0 1.9 %collective-permute-start = (bf16[4,2,2,2,128,128]{5,4,3,2,1,0:T(8,128)(2,1)S(1)}, bf16[4,2,2,2,128,128]{5,4,3,2,1,0:T(8,128)(2,1)}, u32[]{:S(2)}, u32[]{:S(2)}) collective-permute-start(bf16[4,2,2,2,128,128]{5,4,3,2,1,0:T(8,128)(2,1)S(1)} %bitcast.24), channel_id=1, source_target_pairs={{0,16},{1,17},{2,18},{3,19},{4,20},{5,21},{6,22},{7,23},{8,24},{9,... | collective-permute-start | bytes 3145736 | tf_op jit(solution)/shard_map/ppermute | solution.py:36
  33.9 0.0 copy-done.1
  33.9 0.0 copy-start.2
  33.9 1.6 %copy-done.2 = bf16[1,4096,256]{2,1,0:T(8,128)(2,1)S(1)} copy-done((bf16[1,4096,256]{2,1,0:T(8,128)(2,1)S(1)}, bf16[1,4096,256]{2,1,0:T(8,128)(2,1)}, u32[]{:S(2)}) %copy-start.2) | copy-done | bytes 2097176
  35.5 0.0 copy-start.3
  35.5 0.0 copy-start.4
  35.5 0.7 shard_map.76.sum_ref
  36.2 0.4 collective-permute-done.other_ref
  36.7 0.0 copy-done.3
  36.7 0.0 copy-done.4
  36.7 3.5 %shard_map.77 = (bf16[17,256,128]{2,1,0:T(8,128)(2,1)S(1)}, bf16[128,256]{1,0:T(8,128)(2,1)S(1)}, bf16[2,256,256]{2,1,0:T(8,128)(2,1)S(1)}) custom-call(s32[1]{0:T(128)} %bitcast.core_ref, bf16[4,2,2,2,128,128]{5,4,3,2,1,0:T(8,128)(2,1)} %collective-permute-done.other_ref, f32[2,256,256]{2,1,0:T(8,128)S(1)} %shard_map.76.sum_ref, ...), custom_call_target="tpu_custom_call" | custom-call | flops 1073741824 | bytes 4194304 | tf_op jit(solution)/shard_map/pallas_call | solution.py:146
  40.2 2.1 %collective-permute-start.2 = (bf16[17,256,128]{2,1,0:T(8,128)(2,1)S(1)}, bf16[17,256,128]{2,1,0:T(8,128)(2,1)S(1)}, u32[]{:S(2)}, u32[]{:S(2)}) collective-permute-start(bf16[17,256,128]{2,1,0:T(8,128)(2,1)S(1)} %get-tuple-element.7), channel_id=1, source_target_pairs={{0,16},{1,17},{2,18},{3,19},{4,20},{5,21},{6,22},{7,23},{8,24},{9,... | collective-permute-start | bytes 3342344 | tf_op jit(solution)/shard_map/ppermute | solution.py:36
  42.3 0.8 shard_map.78.keep_ref
  43.1 1.8 %collective-permute-done.2.swapped_ref = bf16[17,256,128]{2,1,0:T(8,128)(2,1)S(1)} collective-permute-done((bf16[17,256,128]{2,1,0:T(8,128)(2,1)S(1)}, bf16[17,256,128]{2,1,0:T(8,128)(2,1)S(1)}, u32[]{:S(2)}, u32[]{:S(2)}) %collective-permute-start.2) | collective-permute-done | bytes 1114144 | tf_op jit(solution)/shard_map/ppermute | solution.py:36
  44.9 0.2 shard_map.79
  45.1 19.3 %all_to_all.27 = bf16[16,256,128]{2,1,0:T(8,128)(2,1)S(1)} all-to-all(bf16[16,256,128]{2,1,0:T(8,128)(2,1)S(1)} %bitcast.23), channel_id=1, replica_groups=mesh['zq'=2,'zb'=2,'x'=4,'core'=2,'z_hi'=2,'yq'=4,'yb'=2] {'x','yb','zb'}, dimensions={0} | all-to-all | bytes 2097152 | tf_op jit(solution)/shard_map/all_to_all | solution.py:192
  64.3 0.1 reduce_sum.33
  64.5 16.2 %all_to_all.28 = bf16[4,128,128]{2,1,0:T(8,128)(2,1)S(1)} all-to-all(bf16[4,128,128]{2,1,0:T(8,128)(2,1)S(1)} %bitcast.29), channel_id=1, replica_groups=mesh['zq'=2,'zb'=2,'x'=4,'core'=2,'z_hi'=2,'yq'=4,'yb'=2] {'z_hi','zq'}, dimensions={0} | all-to-all | bytes 262144 | tf_op jit(solution)/shard_map/all_to_all | solution.py:196
  80.8 0.7 broadcast_in_dim.35
  81.5 6.2 %all-to-all-start.4 = ((bf16[8,128,128]{2,1,0:T(8,128)(2,1)}), bf16[8,128,128]{2,1,0:T(8,128)(2,1)S(1)}, u32[]{:S(2)}, u32[]{:S(2)}) async-start(bf16[8,128,128]{2,1,0:T(8,128)(2,1)} %broadcast_in_dim.35), calls=%async_computation.4 | async-start | bytes 524288 | tf_op jit(solution)/shard_map/all_to_all | solution.py:206
  87.7 1.9 %collective-permute-start.1 = (bf16[128,256]{1,0:T(8,128)(2,1)S(1)}, bf16[128,256]{1,0:T(8,128)(2,1)S(1)}, u32[]{:S(2)}, u32[]{:S(2)}) collective-permute-start(bf16[128,256]{1,0:T(8,128)(2,1)S(1)} %get-tuple-element.6), channel_id=1, source_target_pairs={{16,32},{17,33},{18,34},{19,35},{20,36},{21,37},{22,38},{23,39},{2... | collective-permute-start | bytes 196616 | tf_op jit(solution)/shard_map/ppermute | solution.py:44
  89.6 3.6 %collective-permute-done.1 = bf16[128,256]{1,0:T(8,128)(2,1)S(1)} collective-permute-done((bf16[128,256]{1,0:T(8,128)(2,1)S(1)}, bf16[128,256]{1,0:T(8,128)(2,1)S(1)}, u32[]{:S(2)}, u32[]{:S(2)}) %collective-permute-start.1) | collective-permute-done | bytes 65568 | tf_op jit(solution)/shard_map/ppermute | solution.py:44
  93.3 0.7 broadcast_select_fusion
  94.0 4.2 %all-to-all-done.4 = bf16[8,128,128]{2,1,0:T(8,128)(2,1)S(1)} async-done(((bf16[8,128,128]{2,1,0:T(8,128)(2,1)}), bf16[8,128,128]{2,1,0:T(8,128)(2,1)S(1)}, u32[]{:S(2)}, u32[]{:S(2)}) %all-to-all-start.4) | async-done | bytes 262176 | tf_op jit(solution)/shard_map/all_to_all | solution.py:206
  98.2 0.7 convert_reduce_fusion
  (5 shorter events, 0.1 us)
Async XLA Ops:
  0.6 0.8 copy-start
  0.6 33.3 %copy-start.1 = (bf16[1,4096,256]{2,1,0:T(8,128)(2,1)S(1)}, bf16[1,4096,256]{2,1,0:T(8,128)(2,1)}, u32[]{:S(2)}) copy-start(bf16[1,4096,256]{2,1,0:T(8,128)(2,1)} %param.7) | copy-start | bytes 6291460
  32.0 4.7 %collective-permute-start = (bf16[4,2,2,2,128,128]{5,4,3,2,1,0:T(8,128)(2,1)S(1)}, bf16[4,2,2,2,128,128]{5,4,3,2,1,0:T(8,128)(2,1)}, u32[]{:S(2)}, u32[]{:S(2)}) collective-permute-start(bf16[4,2,2,2,128,128]{5,4,3,2,1,0:T(8,128)(2,1)S(1)} %bitcast.24), channel_id=1, source_target_pairs={{0,16},{1,17},{2,18},{3,19},{4,20},{5,21},{6,22},{7,23},{8,24},{9,... | collective-permute-start | bytes 3145736 | tf_op jit(solution)/shard_map/ppermute | solution.py:36
  33.9 1.6 %copy-start.2 = (bf16[1,4096,256]{2,1,0:T(8,128)(2,1)S(1)}, bf16[1,4096,256]{2,1,0:T(8,128)(2,1)}, u32[]{:S(2)}) copy-start(bf16[1,4096,256]{2,1,0:T(8,128)(2,1)} %param.8) | copy-start | bytes 6291460
  35.5 1.2 %copy-start.3 = (bf16[1,2,64,256]{3,2,1,0:T(8,128)(2,1)S(1)}, bf16[1,2,64,256]{3,2,1,0:T(8,128)(2,1)}, u32[]{:S(2)}) copy-start(bf16[1,2,64,256]{3,2,1,0:T(8,128)(2,1)} %param.5) | copy-start | bytes 196612
  35.5 1.2 %copy-start.4 = (bf16[1,2,64,256]{3,2,1,0:T(8,128)(2,1)S(1)}, bf16[1,2,64,256]{3,2,1,0:T(8,128)(2,1)}, u32[]{:S(2)}) copy-start(bf16[1,2,64,256]{3,2,1,0:T(8,128)(2,1)} %param.9) | copy-start | bytes 196612
  40.2 4.6 %collective-permute-start.2 = (bf16[17,256,128]{2,1,0:T(8,128)(2,1)S(1)}, bf16[17,256,128]{2,1,0:T(8,128)(2,1)S(1)}, u32[]{:S(2)}, u32[]{:S(2)}) collective-permute-start(bf16[17,256,128]{2,1,0:T(8,128)(2,1)S(1)} %get-tuple-element.7), channel_id=1, source_target_pairs={{0,16},{1,17},{2,18},{3,19},{4,20},{5,21},{6,22},{7,23},{8,24},{9,... | collective-permute-start | bytes 3342344 | tf_op jit(solution)/shard_map/ppermute | solution.py:36
  81.5 16.7 %all-to-all-start.4 = ((bf16[8,128,128]{2,1,0:T(8,128)(2,1)}), bf16[8,128,128]{2,1,0:T(8,128)(2,1)S(1)}, u32[]{:S(2)}, u32[]{:S(2)}) async-start(bf16[8,128,128]{2,1,0:T(8,128)(2,1)} %broadcast_in_dim.35), calls=%async_computation.4 | async-start | bytes 524288 | tf_op jit(solution)/shard_map/all_to_all | solution.py:206
  87.7 5.6 %collective-permute-start.1 = (bf16[128,256]{1,0:T(8,128)(2,1)S(1)}, bf16[128,256]{1,0:T(8,128)(2,1)S(1)}, u32[]{:S(2)}, u32[]{:S(2)}) collective-permute-start(bf16[128,256]{1,0:T(8,128)(2,1)S(1)} %get-tuple-element.6), channel_id=1, source_target_pairs={{16,32},{17,33},{18,34},{19,35},{20,36},{21,37},{22,38},{23,39},{2... | collective-permute-start | bytes 196616 | tf_op jit(solution)/shard_map/ppermute | solution.py:44

commit v6 on v5

--- a/solution.py
+++ b/solution.py
@@ -6,8 +6,8 @@
 from jax.sharding import Mesh, PartitionSpec as P
 
 HEAD_DIM = 256
-AXES = ("zq", "zb", "x", "core", "z_hi", "yq", "yb")
-SIZES = (2, 2, 4, 2, 2, 4, 2)
+AXES = ("zq", "zb", "xq", "xb", "core", "z_hi", "yq", "yb")
+SIZES = (2, 2, 2, 2, 2, 2, 4, 2)
 CHIPS = 16
 PART = 128
 
@@ -32,6 +32,49 @@
     return pairs
 
 
+FIRST_PAIRS = (((0, 1), (3, 2)), ((1, 2), (0, 3)))
+SECOND_PAIRS = (((0, 3), (1, 2)), ((0, 1), (2, 3)))
+
+
+def exchange(blocks, groups):
+    return lax.all_to_all(blocks, AXES, 0, 0, tiled=True, axis_index_groups=groups)
+
+
+def neighbour_groups():
+    groups = []
+    for core in range(2):
+        for pair_x in FIRST_PAIRS[core]:
+            for y in range(core, 8, 2):
+                for z in range(core, 8, 2):
+                    group = []
+                    for member in range(8):
+                        at_y, at_z = [
+                            (low + (low + (member >> bit)) % 2) % 8 for low, bit in [(y, 1), (z, 0)]
+                        ]
+                        at_x = pair_x[member >> 2]
+                        group.append(index_of(at_z % 4, at_x, core, at_z // 4, at_y))
+                    groups.append(group)
+    return groups
+
+
+def column_groups(both_halves):
+    groups = []
+    for core in range(2):
+        for pair_x in SECOND_PAIRS[core]:
+            for y in range(8):
+                for zb in range(2):
+                    halves = [
+                        [
+                            index_of(2 * zq + zb, at_x, core, z_hi, y)
+                            for zq in range(2)
+                            for at_x in pair_x
+                        ]
+                        for z_hi in range(2)
+                    ]
+                    groups += [halves[0] + halves[1]] if both_halves else halves
+    return groups
+
+
 def to_sibling(block):
     return lax.ppermute(block, AXES, routes(lambda chip, core: (chip, 1 - core)))
 
@@ -54,15 +97,23 @@
     return lax.dot_general(a, b, (contract, ((), ())), preferred_element_type=jnp.float32)
 
 
-def block_of(features, chip):
+def places(chip, core):
     z_lo, x = chip // 4, chip % 4
-    zb, zq = z_lo % 2, z_lo // 2
-    return jnp.concatenate([features[x, 0, zb, zq], features[x, 1, zb, zq]], axis=0)
+    middle = 1 if x in (1, 2) else 0
+    group = jnp.where(core == 0, middle, x // 2)
+    place = jnp.where(core == 0, x // 2, x % 2)
+    return group, z_lo % 2, z_lo // 2, place
+
+
+def block_of(features, chip, core):
+    group, zb, zq, place = places(chip, core)
+    rows = [features[group, half, zb, zq, place] for half in range(2)]
+    return jnp.concatenate(rows, axis=0)
 
 
 def partial_rows(features, key_ref, value_ref, parity, key_sum, value_sum):
     for block in range(CHIPS // 2):
-        sides = [block_of(features, 2 * block), block_of(features, 2 * block + 1)]
+        sides = [block_of(features, 2 * block + side, parity) for side in range(2)]
         tile = jnp.concatenate(sides, axis=1)
         key_part = dot(tile, pair(key_ref, block, parity), ((1,), (0,)))
         value_part = dot(tile, pair(value_ref, block, parity), ((1,), (0,)))
@@ -93,24 +144,27 @@
     )
     key_rows = key_sum.astype(jnp.bfloat16)
     value_rows = value_sum.astype(jnp.bfloat16)
+    micros = range(2)
+    keys = [key_rows[micro * 128:(micro + 1) * 128] for micro in micros]
+    values = [value_rows[micro * 128:(micro + 1) * 128] for micro in micros]
+    scores = [dot(query_ref[micro], keys[micro], ((1,), (1,))) * scale for micro in micros]
+    grad_probs = [dot(grad_ref[micro], values[micro], ((1,), (1,))) for micro in micros]
+    scores = jnp.concatenate(scores, axis=0)
+    grad_probs = jnp.concatenate(grad_probs, axis=0)
+    raised = jnp.exp(scores - jnp.max(scores, axis=-1, keepdims=True))
+    attention = raised / jnp.sum(raised, axis=-1, keepdims=True)
+    prob_low = attention.astype(jnp.bfloat16)
+    row_dot = jnp.sum(attention * grad_probs, axis=-1, keepdims=True)
+    grad_scores = (attention * (grad_probs - row_dot) * scale).astype(jnp.bfloat16)
     contexts, query_grads = [], []
-    for micro in range(2):
-        keys = key_rows[micro * 128:(micro + 1) * 128]
-        values = value_rows[micro * 128:(micro + 1) * 128]
-        query = query_ref[micro]
-        grad = grad_ref[micro]
-        scores = dot(query, keys, ((1,), (1,))) * scale
-        grad_probs = dot(grad, values, ((1,), (1,)))
-        raised = jnp.exp(scores - jnp.max(scores, axis=-1, keepdims=True))
-        attention = raised / jnp.sum(raised, axis=-1, keepdims=True)
-        prob_low = attention.astype(jnp.bfloat16)
-        row_dot = jnp.sum(attention * grad_probs, axis=-1, keepdims=True)
-        grad_scores = (attention * (grad_probs - row_dot) * scale).astype(jnp.bfloat16)
-        contexts.append(dot(prob_low, values, ((1,), (0,))).astype(jnp.bfloat16))
-        query_grads.append(dot(grad_scores, keys, ((1,), (0,))).astype(jnp.bfloat16))
+    for micro in micros:
+        probs = prob_low[micro * 64:(micro + 1) * 64]
+        slopes = grad_scores[micro * 64:(micro + 1) * 64]
         rows = slice(micro * 128, (micro + 1) * 128)
-        grads_ref[0, rows] = dot(grad_scores, query, ((0,), (0,))).astype(jnp.bfloat16)
-        grads_ref[1, rows] = dot(prob_low, grad, ((0,), (0,))).astype(jnp.bfloat16)
+        grads_ref[1, rows] = dot(probs, grad_ref[micro], ((0,), (0,))).astype(jnp.bfloat16)
+        grads_ref[0, rows] = dot(slopes, query_ref[micro], ((0,), (0,))).astype(jnp.bfloat16)
+        contexts.append(dot(probs, values[micro], ((1,), (0,))).astype(jnp.bfloat16))
+        query_grads.append(dot(slopes, keys[micro], ((1,), (0,))).astype(jnp.bfloat16))
     context = jnp.concatenate(contexts, axis=0)
     query_grad = jnp.concatenate(query_grads, axis=0)
     inside = jnp.where(core == 0, context, query_grad)
@@ -133,11 +187,11 @@
 
 def add_kernel(core_ref, keep_ref, swapped_ref, total_ref):
     for chip in range(CHIPS):
-        z_lo, x = chip // 4, chip % 4
+        group, zb, zq, place = places(chip, core_ref[0])
         total = keep_ref[chip] + swapped_ref[chip].astype(jnp.float32)
         total = total.astype(jnp.bfloat16)
-        total_ref[x, 0, z_lo % 2, z_lo // 2] = total[:128]
-        total_ref[x, 1, z_lo % 2, z_lo // 2] = total[128:]
+        total_ref[group, 0, zb, zq, place] = total[:128]
+        total_ref[group, 1, zb, zq, place] = total[128:]
 
 
 def call(kernel, outs, flops, *args):
@@ -159,11 +213,10 @@
     key_layer, value_layer = key_weight[0], value_weight[0]
     low, full = jnp.bfloat16, jnp.float32
     half = lax.dynamic_slice_in_dim(memory, lax.axis_index("yb"), 1, 0)
-    column = lax.all_to_all(jnp.broadcast_to(half, (2, 128, PART)), "zq", 0, 0, tiled=True)
-    mine = lax.all_to_all(
-        jnp.broadcast_to(column.reshape(1, 256, PART), (16, 256, PART)),
-        ("x", "yb", "zb"), 0, 0, tiled=True,
-    ).reshape(4, 2, 2, 2, 128, PART)
+    column = exchange(jnp.broadcast_to(half, (4, 128, PART)), column_groups(False))
+    mine = exchange(
+        jnp.broadcast_to(column.reshape(1, 512, PART), (8, 512, PART)), neighbour_groups()
+    ).reshape(2, 2, 2, 2, 2, 128, PART)
     other = to_sibling(mine)
     (sums,) = call(
         begin_kernel, [jax.ShapeDtypeStruct((2, 256, 256), full)], 2**29,
@@ -186,16 +239,13 @@
         core_at, grads, key_layer, value_layer,
     )
     (chip_sum,) = call(
-        add_kernel, [jax.ShapeDtypeStruct((4, 2, 2, 2, 128, PART), low)], 2**20,
+        add_kernel, [jax.ShapeDtypeStruct((2, 2, 2, 2, 2, 128, PART), low)], 2**20,
         core_at, keep, swapped,
     )
-    pieces = lax.all_to_all(
-        chip_sum.reshape(16, 256, PART), ("x", "yb", "zb"), 0, 0, tiled=True
-    )
-    piece = jnp.sum(pieces.astype(full), axis=0).astype(low).reshape(1, 2, 128, PART)
-    pieces = lax.all_to_all(
-        jnp.broadcast_to(piece, (2, 2, 128, PART)).reshape(4, 128, PART),
-        ("z_hi", "zq"), 0, 0, tiled=True,
+    pieces = exchange(chip_sum.reshape(8, 512, PART), neighbour_groups())
+    piece = jnp.sum(pieces.astype(full), axis=0).astype(low).reshape(1, 4, 128, PART)
+    pieces = exchange(
+        jnp.broadcast_to(piece, (2, 4, 128, PART)).reshape(8, 128, PART), column_groups(True)
     )
     inside = swapped[CHIPS].reshape(2, 2, 64, PART)
     got_inside = jnp.concatenate([inside[0], inside[1]], axis=-1)
@@ -212,7 +262,7 @@
 
 def solution(mesh):
     fine = Mesh(mesh.devices.reshape(SIZES), AXES)
-    section = ("zq", "zb", "x", "core")
+    section = ("zq", "zb", "xq", "xb", "core")
     mp = ("z_hi", "yq", "yb")
     in_specs = (
         P(section, None, None, mp),

time: 99.9 us -> 98.2 us (0.983)
  blocking collectives: 65.8 us -> 58.7 us
  starting transfers between devices: 12.1 us -> 17.1 us
  waiting for transfers between devices: 10.1 us -> 11.2 us
    all_to_all x4, blocking collectives: 65.8 us -> 58.7 us  [exchange(): lax.all_to_all(blocks, AXES, 0, 0, tiled=True, axis_index_groups=groups)]
    ppermute x2, starting transfers between devices: 4.03 us -> 9.13 us  [to_sibling(): lax.ppermute(block, AXES, routes(lambda chip, core: (chip, 1 - core)))]
    all_to_all x1, waiting for transfers between devices: 4.23 us -> 5.79 us  [per_device(): lax.all_to_all(jnp.broadcast_to(piece[None], (8, 128, PART)), ('yq', 'yb'...]
  transfers between devices with their start and end apart: 4 -> 4, of which waited for: 4 -> 4; matrix products, arithmetic and copies ran while one was open for 1% -> 1% of each run, Pallas kernels for 1% -> 2%
where the time goes in v6:
time: 98.2 us; the launch traced here: 97.6 us
  blocking collectives  58.7 us (60%)
  starting transfers between devices  17.1 us (17%)
  waiting for transfers between devices  11.2 us (11%)
  Pallas kernels  4.94 us (5%)
  local copies, waits for them, and re-layouts  3.43 us (3%)
  other arithmetic  1.55 us (2%)
    all_to_all x4, blocking collectives, exchange(): lax.all_to_all(blocks, AXES, 0, 0, tiled=True, axis_index_groups=groups)  58.7 us
    ppermute x2, starting transfers between devices, to_sibling(): lax.ppermute(block, AXES, routes(lambda chip, core: (chip, 1 - core)))  9.13 us
    all_to_all x1, starting transfers between devices, per_device(): lax.all_to_all(jnp.broadcast_to(piece[None], (8, 128, PART)), ('yq', 'yb'...  6.02 us
    all_to_all x1, waiting for transfers between devices, per_device(): lax.all_to_all(jnp.broadcast_to(piece[None], (8, 128, PART)), ('yq', 'yb'...  5.79 us
    pallas_call x4, Pallas kernels, call(): pl.pallas_call(kernel, out_shape=outs, in_specs=specs, out_specs=[pl.Bloc...  4.94 us
    ppermute x1, waiting for transfers between devices, to_next_chip(): return lax.ppermute(block, AXES, routes(step))  3.64 us
    unnamed x10, local copies, waits for them, and re-layouts  2.5 us
  transfers between devices with their start and end apart: 4, of which 4 were waited for; matrix products, arithmetic and copies ran while one was open for 1% of the time, Pallas kernels for 2%

profile of v6, /device:TPU:6, one launch (start us, length us, event | category | flops | bytes accessed | tf_op | source)
XLA Modules:
  0.0 97.6 jit_solution(4565054150020795115)
XLA Ops:
  0.6 0.0 copy-start
  0.6 0.0 copy-start.1
  0.7 0.8 copy-done
  1.5 13.0 %all_to_all.25 = bf16[4,128,128]{2,1,0:T(8,128)(2,1)S(1)} all-to-all(bf16[4,128,128]{2,1,0:T(8,128)(2,1)S(1)} %broadcast_in_dim.30), channel_id=1, replica_groups={{0,96,256,352},{8,104,264,360},{128,224,384,480},{136,232,392,488},{1,9..., dimensions={0} | all-to-all | bytes 262144 | tf_op jit(solution)/shard_map/all_to_all | solution.py:40
  14.6 0.1 broadcast_in_dim.32
  14.7 15.3 %all_to_all.26 = bf16[8,512,128]{2,1,0:T(8,128)(2,1)S(1)} all-to-all(bf16[8,512,128]{2,1,0:T(8,128)(2,1)S(1)} %broadcast_in_dim.32), channel_id=1, replica_groups={{0,128,1,129,32,160,33,161},{256,384,257,385,288,416,289,417},{8,136,9,..., dimensions={0} | all-to-all | bytes 2097152 | tf_op jit(solution)/shard_map/all_to_all | solution.py:40
  30.0 6.9 %collective-permute-start = (bf16[2,2,2,2,2,128,128]{6,5,4,3,2,1,0:T(8,128)(2,1)S(1)}, bf16[2,2,2,2,2,128,128]{6,5,4,3,2,1,0:T(8,128)(2,1)}, u32[]{:S(2)}, u32[]{:S(2)}) collective-permute-start(bf16[2,2,2,2,2,128,128]{6,5,4,3,2,1,0:T(8,128)(2,1)S(1)} %bitcast.24), channel_id=1, source_target_pairs={{0,16},{1,17},{2,18},{3,19},{4,20},{5,21},{6,22},{7,23},{8,24},{9,... | collective-permute-start | bytes 3145736 | tf_op jit(solution)/shard_map/ppermute | solution.py:79
  37.0 0.0 copy-done.1
  37.0 0.0 copy-start.2
  37.0 1.6 %copy-done.2 = bf16[1,4096,256]{2,1,0:T(8,128)(2,1)S(1)} copy-done((bf16[1,4096,256]{2,1,0:T(8,128)(2,1)S(1)}, bf16[1,4096,256]{2,1,0:T(8,128)(2,1)}, u32[]{:S(2)}) %copy-start.2) | copy-done | bytes 2097176
  38.6 0.0 copy-start.3
  38.6 0.0 copy-start.4
  38.6 0.7 shard_map.76.sum_ref
  39.3 0.1 collective-permute-done.other_ref
  39.4 0.1 copy-done.3
  39.4 0.0 copy-done.4
  39.4 3.3 %shard_map.77 = (bf16[17,256,128]{2,1,0:T(8,128)(2,1)S(1)}, bf16[128,256]{1,0:T(8,128)(2,1)S(1)}, bf16[2,256,256]{2,1,0:T(8,128)(2,1)S(1)}) custom-call(s32[1]{0:T(128)} %bitcast.core_ref, bf16[2,2,2,2,2,128,128]{6,5,4,3,2,1,0:T(8,128)(2,1)} %collective-permute-done.other_ref, f32[2,256,256]{2,1,0:T(8,128)S(1)} %shard_map.76.sum_ref, ...), custom_call_target="tpu_custom_call" | custom-call | flops 1073741824 | bytes 4194304 | tf_op jit(solution)/shard_map/pallas_call | solution.py:200
  42.7 2.2 %collective-permute-start.2 = (bf16[17,256,128]{2,1,0:T(8,128)(2,1)S(1)}, bf16[17,256,128]{2,1,0:T(8,128)(2,1)S(1)}, u32[]{:S(2)}, u32[]{:S(2)}) collective-permute-start(bf16[17,256,128]{2,1,0:T(8,128)(2,1)S(1)} %get-tuple-element.7), channel_id=1, source_target_pairs={{0,16},{1,17},{2,18},{3,19},{4,20},{5,21},{6,22},{7,23},{8,24},{9,... | collective-permute-start | bytes 3342344 | tf_op jit(solution)/shard_map/ppermute | solution.py:79
  44.9 0.7 shard_map.78.keep_ref
  45.7 1.7 %collective-permute-done.2.swapped_ref = bf16[17,256,128]{2,1,0:T(8,128)(2,1)S(1)} collective-permute-done((bf16[17,256,128]{2,1,0:T(8,128)(2,1)S(1)}, bf16[17,256,128]{2,1,0:T(8,128)(2,1)S(1)}, u32[]{:S(2)}, u32[]{:S(2)}) %collective-permute-start.2) | collective-permute-done | bytes 1114144 | tf_op jit(solution)/shard_map/ppermute | solution.py:79
  47.4 0.2 shard_map.79
  47.6 13.6 %all_to_all.27 = bf16[8,512,128]{2,1,0:T(8,128)(2,1)S(1)} all-to-all(bf16[8,512,128]{2,1,0:T(8,128)(2,1)S(1)} %bitcast.23), channel_id=1, replica_groups={{0,128,1,129,32,160,33,161},{256,384,257,385,288,416,289,417},{8,136,9,..., dimensions={0} | all-to-all | bytes 2097152 | tf_op jit(solution)/shard_map/all_to_all | solution.py:40
  61.2 0.1 reduce_sum.33
  61.4 16.7 %all_to_all.28 = bf16[8,128,128]{2,1,0:T(8,128)(2,1)S(1)} all-to-all(bf16[8,128,128]{2,1,0:T(8,128)(2,1)S(1)} %bitcast.29), channel_id=1, replica_groups={{0,96,256,352,8,104,264,360},{128,224,384,480,136,232,392,488},{1,97,25..., dimensions={0} | all-to-all | bytes 524288 | tf_op jit(solution)/shard_map/all_to_all | solution.py:40
  78.1 0.7 broadcast_in_dim.35
  78.9 6.0 %all-to-all-start.4 = ((bf16[8,128,128]{2,1,0:T(8,128)(2,1)}), bf16[8,128,128]{2,1,0:T(8,128)(2,1)S(1)}, u32[]{:S(2)}, u32[]{:S(2)}) async-start(bf16[8,128,128]{2,1,0:T(8,128)(2,1)} %broadcast_in_dim.35), calls=%async_computation.4 | async-start | bytes 524288 | tf_op jit(solution)/shard_map/all_to_all | solution.py:256
  84.9 1.9 %collective-permute-start.1 = (bf16[128,256]{1,0:T(8,128)(2,1)S(1)}, bf16[128,256]{1,0:T(8,128)(2,1)S(1)}, u32[]{:S(2)}, u32[]{:S(2)}) collective-permute-start(bf16[128,256]{1,0:T(8,128)(2,1)S(1)} %get-tuple-element.6), channel_id=1, source_target_pairs={{16,32},{17,33},{18,34},{19,35},{20,36},{21,37},{22,38},{23,39},{2... | collective-permute-start | bytes 196616 | tf_op jit(solution)/shard_map/ppermute | solution.py:87
  86.8 3.6 %collective-permute-done.1 = bf16[128,256]{1,0:T(8,128)(2,1)S(1)} collective-permute-done((bf16[128,256]{1,0:T(8,128)(2,1)S(1)}, bf16[128,256]{1,0:T(8,128)(2,1)S(1)}, u32[]{:S(2)}, u32[]{:S(2)}) %collective-permute-start.1) | collective-permute-done | bytes 65568 | tf_op jit(solution)/shard_map/ppermute | solution.py:87
  90.5 0.7 broadcast_select_fusion
  91.1 5.8 %all-to-all-done.4 = bf16[8,128,128]{2,1,0:T(8,128)(2,1)S(1)} async-done(((bf16[8,128,128]{2,1,0:T(8,128)(2,1)}), bf16[8,128,128]{2,1,0:T(8,128)(2,1)S(1)}, u32[]{:S(2)}, u32[]{:S(2)}) %all-to-all-start.4) | async-done | bytes 262176 | tf_op jit(solution)/shard_map/all_to_all | solution.py:256
  96.9 0.7 convert_reduce_fusion
  (5 shorter events, 0.1 us)
Async XLA Ops:
  0.6 0.8 copy-start
  0.6 36.3 %copy-start.1 = (bf16[1,4096,256]{2,1,0:T(8,128)(2,1)S(1)}, bf16[1,4096,256]{2,1,0:T(8,128)(2,1)}, u32[]{:S(2)}) copy-start(bf16[1,4096,256]{2,1,0:T(8,128)(2,1)} %param.7) | copy-start | bytes 6291460
  30.0 9.3 %collective-permute-start = (bf16[2,2,2,2,2,128,128]{6,5,4,3,2,1,0:T(8,128)(2,1)S(1)}, bf16[2,2,2,2,2,128,128]{6,5,4,3,2,1,0:T(8,128)(2,1)}, u32[]{:S(2)}, u32[]{:S(2)}) collective-permute-start(bf16[2,2,2,2,2,128,128]{6,5,4,3,2,1,0:T(8,128)(2,1)S(1)} %bitcast.24), channel_id=1, source_target_pairs={{0,16},{1,17},{2,18},{3,19},{4,20},{5,21},{6,22},{7,23},{8,24},{9,... | collective-permute-start | bytes 3145736 | tf_op jit(solution)/shard_map/ppermute | solution.py:79
  37.0 1.6 %copy-start.2 = (bf16[1,4096,256]{2,1,0:T(8,128)(2,1)S(1)}, bf16[1,4096,256]{2,1,0:T(8,128)(2,1)}, u32[]{:S(2)}) copy-start(bf16[1,4096,256]{2,1,0:T(8,128)(2,1)} %param.8) | copy-start | bytes 6291460
  38.6 0.8 copy-start.3
  38.6 0.9 copy-start.4
  42.7 4.6 %collective-permute-start.2 = (bf16[17,256,128]{2,1,0:T(8,128)(2,1)S(1)}, bf16[17,256,128]{2,1,0:T(8,128)(2,1)S(1)}, u32[]{:S(2)}, u32[]{:S(2)}) collective-permute-start(bf16[17,256,128]{2,1,0:T(8,128)(2,1)S(1)} %get-tuple-element.7), channel_id=1, source_target_pairs={{0,16},{1,17},{2,18},{3,19},{4,20},{5,21},{6,22},{7,23},{8,24},{9,... | collective-permute-start | bytes 3342344 | tf_op jit(solution)/shard_map/ppermute | solution.py:79
  78.9 18.1 %all-to-all-start.4 = ((bf16[8,128,128]{2,1,0:T(8,128)(2,1)}), bf16[8,128,128]{2,1,0:T(8,128)(2,1)S(1)}, u32[]{:S(2)}, u32[]{:S(2)}) async-start(bf16[8,128,128]{2,1,0:T(8,128)(2,1)} %broadcast_in_dim.35), calls=%async_computation.4 | async-start | bytes 524288 | tf_op jit(solution)/shard_map/all_to_all | solution.py:256
  84.9 5.6 %collective-permute-start.1 = (bf16[128,256]{1,0:T(8,128)(2,1)S(1)}, bf16[128,256]{1,0:T(8,128)(2,1)S(1)}, u32[]{:S(2)}, u32[]{:S(2)}) collective-permute-start(bf16[128,256]{1,0:T(8,128)(2,1)S(1)} %get-tuple-element.6), channel_id=1, source_target_pairs={{16,32},{17,33},{18,34},{19,35},{20,36},{21,37},{22,38},{23,39},{2... | collective-permute-start | bytes 196616 | tf_op jit(solution)/shard_map/ppermute | solution.py:87

commit v7 on v6

--- a/solution.py
+++ b/solution.py
@@ -194,6 +194,24 @@
         total_ref[group, 1, zb, zq, place] = total[128:]
 
 
+def output_kernel(
+    core_ref, swapped_ref, across_ref, whole_ref, context_ref, query_ref, memory_ref
+):
+    core = core_ref[0]
+    inside = jnp.concatenate([swapped_ref[CHIPS, :128], swapped_ref[CHIPS, 128:]], axis=1)
+    across = across_ref[...]
+    context = jnp.where(core == 0, across, inside)
+    query_grad = jnp.where(core == 0, inside, across)
+    for micro in range(2):
+        rows = slice(micro * 64, (micro + 1) * 64)
+        context_ref[0, micro] = context[rows]
+        query_ref[0, micro] = query_grad[rows]
+        total = whole_ref[micro].astype(jnp.float32)
+        for pairs in range(1, 4):
+            total = total + whole_ref[2 * pairs + micro].astype(jnp.float32)
+        memory_ref[micro] = total
+
+
 def call(kernel, outs, flops, *args):
     specs = [pl.BlockSpec(memory_space=pltpu.SMEM)]
     specs += [pl.BlockSpec(memory_space=pltpu.VMEM)] * (len(args) - 1)
@@ -247,17 +265,20 @@
     pieces = exchange(
         jnp.broadcast_to(piece, (2, 4, 128, PART)).reshape(8, 128, PART), column_groups(True)
     )
-    inside = swapped[CHIPS].reshape(2, 2, 64, PART)
-    got_inside = jnp.concatenate([inside[0], inside[1]], axis=-1)
-    got_across = got_across.reshape(2, 64, 256)
-    passed_context = jnp.where(core == 0, got_across, got_inside)
-    passed_query_grad = jnp.where(core == 0, got_inside, got_across)
     piece = jnp.sum(pieces.astype(full), axis=0).astype(low)
     whole = lax.all_to_all(
         jnp.broadcast_to(piece[None], (8, 128, PART)), ("yq", "yb"), 0, 0, tiled=True
     )
-    memory_grad = jnp.sum(whole.reshape(4, 2, 128, PART).astype(full), axis=0)
-    return (passed_context[None], passed_query_grad[None], memory_grad)
+    passed_context, passed_query_grad, memory_grad = call(
+        output_kernel,
+        [
+            jax.ShapeDtypeStruct((1, 2, 64, 256), low),
+            jax.ShapeDtypeStruct((1, 2, 64, 256), low),
+            jax.ShapeDtypeStruct((2, 128, PART), full),
+        ],
+        2**20, core_at, swapped, got_across, whole,
+    )
+    return (passed_context, passed_query_grad, memory_grad)
 
 
 def solution(mesh):

time: 98.2 us -> 98.2 us (level)
  other arithmetic: 1.55 us -> 0.19 us
    pallas_call x4 -> x5, Pallas kernels: 4.94 us -> 5.66 us  [call(): pl.pallas_call(kernel, out_shape=outs, in_specs=specs, out_specs=[pl.Bloc...]
  transfers between devices with their start and end apart: 4 -> 4, of which waited for: 4 -> 4; matrix products, arithmetic and copies ran while one was open for 1% -> 0% of each run, Pallas kernels for 2% -> 2%
where the time goes in v7:
time: 98.2 us; the launch traced here: 97.6 us
  blocking collectives  58.7 us (60%)
  starting transfers between devices  17.1 us (17%)
  waiting for transfers between devices  11.9 us (12%)
  Pallas kernels  5.66 us (6%)
  local copies, waits for them, and re-layouts  3.43 us (3%)
    all_to_all x4, blocking collectives, exchange(): lax.all_to_all(blocks, AXES, 0, 0, tiled=True, axis_index_groups=groups)  58.7 us
    ppermute x2, starting transfers between devices, to_sibling(): lax.ppermute(block, AXES, routes(lambda chip, core: (chip, 1 - core)))  9.13 us
    all_to_all x1, waiting for transfers between devices, per_device(): lax.all_to_all(jnp.broadcast_to(piece[None], (8, 128, PART)), ('yq', 'yb'...  6.47 us
    all_to_all x1, starting transfers between devices, per_device(): lax.all_to_all(jnp.broadcast_to(piece[None], (8, 128, PART)), ('yq', 'yb'...  6.02 us
    pallas_call x5, Pallas kernels, call(): pl.pallas_call(kernel, out_shape=outs, in_specs=specs, out_specs=[pl.Bloc...  5.66 us
    ppermute x1, waiting for transfers between devices, to_next_chip(): return lax.ppermute(block, AXES, routes(step))  3.66 us
    unnamed x10, local copies, waits for them, and re-layouts  2.5 us
  transfers between devices with their start and end apart: 4, of which 4 were waited for; matrix products, arithmetic and copies ran while one was open for 0% of the time, Pallas kernels for 2%

profile of v7, /device:TPU:6, one launch (start us, length us, event | category | flops | bytes accessed | tf_op | source)
XLA Modules:
  0.0 97.6 jit_solution(4730358740846029813)
XLA Ops:
  0.6 0.0 copy-start
  0.6 0.0 copy-start.1
  0.7 0.8 copy-done
  1.5 13.0 %all_to_all.25 = bf16[4,128,128]{2,1,0:T(8,128)(2,1)S(1)} all-to-all(bf16[4,128,128]{2,1,0:T(8,128)(2,1)S(1)} %broadcast_in_dim.28), channel_id=1, replica_groups={{0,96,256,352},{8,104,264,360},{128,224,384,480},{136,232,392,488},{1,9..., dimensions={0} | all-to-all | bytes 262144 | tf_op jit(solution)/shard_map/all_to_all | solution.py:40
  14.6 0.1 broadcast_in_dim.30
  14.7 15.3 %all_to_all.26 = bf16[8,512,128]{2,1,0:T(8,128)(2,1)S(1)} all-to-all(bf16[8,512,128]{2,1,0:T(8,128)(2,1)S(1)} %broadcast_in_dim.30), channel_id=1, replica_groups={{0,128,1,129,32,160,33,161},{256,384,257,385,288,416,289,417},{8,136,9,..., dimensions={0} | all-to-all | bytes 2097152 | tf_op jit(solution)/shard_map/all_to_all | solution.py:40
  30.0 6.9 %collective-permute-start = (bf16[2,2,2,2,2,128,128]{6,5,4,3,2,1,0:T(8,128)(2,1)S(1)}, bf16[2,2,2,2,2,128,128]{6,5,4,3,2,1,0:T(8,128)(2,1)}, u32[]{:S(2)}, u32[]{:S(2)}) collective-permute-start(bf16[2,2,2,2,2,128,128]{6,5,4,3,2,1,0:T(8,128)(2,1)S(1)} %bitcast.19), channel_id=1, source_target_pairs={{0,16},{1,17},{2,18},{3,19},{4,20},{5,21},{6,22},{7,23},{8,24},{9,... | collective-permute-start | bytes 3145736 | tf_op jit(solution)/shard_map/ppermute | solution.py:79
  37.0 0.0 copy-done.1
  37.0 0.0 copy-start.2
  37.0 1.6 %copy-done.2 = bf16[1,4096,256]{2,1,0:T(8,128)(2,1)S(1)} copy-done((bf16[1,4096,256]{2,1,0:T(8,128)(2,1)S(1)}, bf16[1,4096,256]{2,1,0:T(8,128)(2,1)}, u32[]{:S(2)}) %copy-start.2) | copy-done | bytes 2097176
  38.6 0.0 copy-start.3
  38.6 0.0 copy-start.4
  38.6 0.7 shard_map.76.sum_ref
  39.3 0.1 collective-permute-done.other_ref
  39.4 0.1 copy-done.3
  39.4 0.0 copy-done.4
  39.4 3.3 %shard_map.77 = (bf16[17,256,128]{2,1,0:T(8,128)(2,1)S(1)}, bf16[128,256]{1,0:T(8,128)(2,1)S(1)}, bf16[2,256,256]{2,1,0:T(8,128)(2,1)S(1)}) custom-call(s32[1]{0:T(128)} %bitcast.core_ref, bf16[2,2,2,2,2,128,128]{6,5,4,3,2,1,0:T(8,128)(2,1)} %collective-permute-done.other_ref, f32[2,256,256]{2,1,0:T(8,128)S(1)} %shard_map.76.sum_ref, ...), custom_call_target="tpu_custom_call" | custom-call | flops 1073741824 | bytes 4194304 | tf_op jit(solution)/shard_map/pallas_call | solution.py:218
  42.7 2.2 %collective-permute-start.1 = (bf16[17,256,128]{2,1,0:T(8,128)(2,1)S(1)}, bf16[17,256,128]{2,1,0:T(8,128)(2,1)S(1)}, u32[]{:S(2)}, u32[]{:S(2)}) collective-permute-start(bf16[17,256,128]{2,1,0:T(8,128)(2,1)S(1)} %get-tuple-element.6), channel_id=1, source_target_pairs={{0,16},{1,17},{2,18},{3,19},{4,20},{5,21},{6,22},{7,23},{8,24},{9,... | collective-permute-start | bytes 3342344 | tf_op jit(solution)/shard_map/ppermute | solution.py:79
  44.9 0.7 shard_map.78.keep_ref
  45.7 1.7 %collective-permute-done.1.swapped_ref = bf16[17,256,128]{2,1,0:T(8,128)(2,1)S(1)} collective-permute-done((bf16[17,256,128]{2,1,0:T(8,128)(2,1)S(1)}, bf16[17,256,128]{2,1,0:T(8,128)(2,1)S(1)}, u32[]{:S(2)}, u32[]{:S(2)}) %collective-permute-start.1) | collective-permute-done | bytes 1114144 | tf_op jit(solution)/shard_map/ppermute | solution.py:79
  47.4 0.2 shard_map.79
  47.6 13.6 %all_to_all.27 = bf16[8,512,128]{2,1,0:T(8,128)(2,1)S(1)} all-to-all(bf16[8,512,128]{2,1,0:T(8,128)(2,1)S(1)} %bitcast.18), channel_id=1, replica_groups={{0,128,1,129,32,160,33,161},{256,384,257,385,288,416,289,417},{8,136,9,..., dimensions={0} | all-to-all | bytes 2097152 | tf_op jit(solution)/shard_map/all_to_all | solution.py:40
  61.2 0.1 reduce_sum.24
  61.4 16.7 %all_to_all.28 = bf16[8,128,128]{2,1,0:T(8,128)(2,1)S(1)} all-to-all(bf16[8,128,128]{2,1,0:T(8,128)(2,1)S(1)} %bitcast.23), channel_id=1, replica_groups={{0,96,256,352,8,104,264,360},{128,224,384,480,136,232,392,488},{1,97,25..., dimensions={0} | all-to-all | bytes 524288 | tf_op jit(solution)/shard_map/all_to_all | solution.py:40
  78.1 0.7 broadcast_in_dim.33
  78.9 6.0 %all-to-all-start.4 = ((bf16[8,128,128]{2,1,0:T(8,128)(2,1)}), bf16[8,128,128]{2,1,0:T(8,128)(2,1)S(1)}, u32[]{:S(2)}, u32[]{:S(2)}) async-start(bf16[8,128,128]{2,1,0:T(8,128)(2,1)} %broadcast_in_dim.33), calls=%async_computation.4 | async-start | bytes 524288 | tf_op jit(solution)/shard_map/all_to_all | solution.py:269
  84.9 1.9 %collective-permute-start.2 = (bf16[128,256]{1,0:T(8,128)(2,1)S(1)}, bf16[128,256]{1,0:T(8,128)(2,1)S(1)}, u32[]{:S(2)}, u32[]{:S(2)}) collective-permute-start(bf16[128,256]{1,0:T(8,128)(2,1)S(1)} %get-tuple-element.7), channel_id=1, source_target_pairs={{16,32},{17,33},{18,34},{19,35},{20,36},{21,37},{22,38},{23,39},{2... | collective-permute-start | bytes 196616 | tf_op jit(solution)/shard_map/ppermute | solution.py:87
  86.8 3.7 %collective-permute-done.2.across_ref = bf16[128,256]{1,0:T(8,128)(2,1)S(1)} collective-permute-done((bf16[128,256]{1,0:T(8,128)(2,1)S(1)}, bf16[128,256]{1,0:T(8,128)(2,1)S(1)}, u32[]{:S(2)}, u32[]{:S(2)}) %collective-permute-start.2) | collective-permute-done | bytes 65568 | tf_op jit(solution)/shard_map/ppermute | solution.py:87
  90.5 6.5 %all-to-all-done.4.whole_ref = bf16[8,128,128]{2,1,0:T(8,128)(2,1)S(1)} async-done(((bf16[8,128,128]{2,1,0:T(8,128)(2,1)}), bf16[8,128,128]{2,1,0:T(8,128)(2,1)S(1)}, u32[]{:S(2)}, u32[]{:S(2)}) %all-to-all-start.4) | async-done | bytes 262176 | tf_op jit(solution)/shard_map/all_to_all | solution.py:269
  96.9 0.7 shard_map.80
  (4 shorter events, 0.1 us)
Async XLA Ops:
  0.6 0.8 copy-start
  0.6 36.3 %copy-start.1 = (bf16[1,4096,256]{2,1,0:T(8,128)(2,1)S(1)}, bf16[1,4096,256]{2,1,0:T(8,128)(2,1)}, u32[]{:S(2)}) copy-start(bf16[1,4096,256]{2,1,0:T(8,128)(2,1)} %param.7) | copy-start | bytes 6291460
  30.0 9.3 %collective-permute-start = (bf16[2,2,2,2,2,128,128]{6,5,4,3,2,1,0:T(8,128)(2,1)S(1)}, bf16[2,2,2,2,2,128,128]{6,5,4,3,2,1,0:T(8,128)(2,1)}, u32[]{:S(2)}, u32[]{:S(2)}) collective-permute-start(bf16[2,2,2,2,2,128,128]{6,5,4,3,2,1,0:T(8,128)(2,1)S(1)} %bitcast.19), channel_id=1, source_target_pairs={{0,16},{1,17},{2,18},{3,19},{4,20},{5,21},{6,22},{7,23},{8,24},{9,... | collective-permute-start | bytes 3145736 | tf_op jit(solution)/shard_map/ppermute | solution.py:79
  37.0 1.6 %copy-start.2 = (bf16[1,4096,256]{2,1,0:T(8,128)(2,1)S(1)}, bf16[1,4096,256]{2,1,0:T(8,128)(2,1)}, u32[]{:S(2)}) copy-start(bf16[1,4096,256]{2,1,0:T(8,128)(2,1)} %param.8) | copy-start | bytes 6291460
  38.6 0.8 copy-start.3
  38.6 0.9 copy-start.4
  42.7 4.6 %collective-permute-start.1 = (bf16[17,256,128]{2,1,0:T(8,128)(2,1)S(1)}, bf16[17,256,128]{2,1,0:T(8,128)(2,1)S(1)}, u32[]{:S(2)}, u32[]{:S(2)}) collective-permute-start(bf16[17,256,128]{2,1,0:T(8,128)(2,1)S(1)} %get-tuple-element.6), channel_id=1, source_target_pairs={{0,16},{1,17},{2,18},{3,19},{4,20},{5,21},{6,22},{7,23},{8,24},{9,... | collective-permute-start | bytes 3342344 | tf_op jit(solution)/shard_map/ppermute | solution.py:79
  78.9 18.1 %all-to-all-start.4 = ((bf16[8,128,128]{2,1,0:T(8,128)(2,1)}), bf16[8,128,128]{2,1,0:T(8,128)(2,1)S(1)}, u32[]{:S(2)}, u32[]{:S(2)}) async-start(bf16[8,128,128]{2,1,0:T(8,128)(2,1)} %broadcast_in_dim.33), calls=%async_computation.4 | async-start | bytes 524288 | tf_op jit(solution)/shard_map/all_to_all | solution.py:269
  84.9 5.6 %collective-permute-start.2 = (bf16[128,256]{1,0:T(8,128)(2,1)S(1)}, bf16[128,256]{1,0:T(8,128)(2,1)S(1)}, u32[]{:S(2)}, u32[]{:S(2)}) collective-permute-start(bf16[128,256]{1,0:T(8,128)(2,1)S(1)} %get-tuple-element.7), channel_id=1, source_target_pairs={{16,32},{17,33},{18,34},{19,35},{20,36},{21,37},{22,38},{23,39},{2... | collective-permute-start | bytes 196616 | tf_op jit(solution)/shard_map/ppermute | solution.py:87
